TPU v7x, 256 devices: a whole 4x4x8 slice. The times are simulated.
256 devices in a mesh: layer: 4 (over z_lo), vocab: 16 (over y, x), dp: 4 (over z_hi, core).
Axes of the slice: x: 4, y: 4, z: 8 (z_hi: 2, z_lo: 4; z = z_hi * 4 + z_lo), core: 2. Of those that a mesh axis runs over, the one named last changes fastest.
Arguments:
- hidden: bfloat16 [4, 512, 4096], P('layer', None, 'vocab'), may hold values from -50 to 50
- translator: bfloat16 [4, 4096, 4096], P('layer', 'vocab', 'dp'), may hold values from -3 to 3
- bias: float32 [4, 4096], P('layer', 'dp'), may hold values from -12 to 12
- gain: float32 [4096], P('dp'), may hold values from 0.5 to 1.5
- head: bfloat16 [4096, 65536], P('dp', 'vocab'), may hold values from -8 to 8
- final_logits: bfloat16 [4, 128, 65536], P('dp', 'layer', 'vocab'), may hold values from -20 to 310
Outputs:
- grad_translator: float32 [4, 4096, 4096], P('layer', 'vocab', 'dp')
- grad_bias: float32 [4, 4096], P('layer', 'dp')
- divergence: float32 [4], P('layer')
All inputs are finite; a program needn't handle non-finite values.
Results may differ from a plain program's by a relative error of at most 0.0065.
Values may be sent and summed in bfloat16 or wider, within the bound.
A program may use at most 64 MiB of HBM per device.

v0:
```python
import jax
import jax.numpy as jnp
from jax import lax
from jax.sharding import PartitionSpec as P

D = 4096


epsilon = 1e-05


def shards(hidden, translator, bias, gain, head, final_logits):
    features = hidden[0]
    weights = translator[0]
    offsets = bias[0]
    token_count = features.shape[0]
    model_width = D
    vocab_groups = lax.axis_size("vocab")
    target_logits = lax.all_gather(final_logits, "layer", axis=1, tiled=True)[0].astype(jnp.float32)
    projected = (
        lax.psum(jnp.dot(features, weights, preferred_element_type=jnp.float32), "vocab") + offsets
    )
    squares = lax.psum(jnp.sum(projected * projected, axis=1), "dp")
    inverse = lax.rsqrt(squares / model_width + epsilon)
    scaled = projected * inverse[:, None]
    normed_here = (scaled * gain).astype(jnp.bfloat16)
    logits = lax.psum_scatter(
        jnp.dot(normed_here, head, preferred_element_type=jnp.float32),
        "dp",
        scatter_dimension=0,
        tiled=True,
    )
    target_top = jnp.max(target_logits, axis=1)
    logit_top = jnp.max(logits, axis=1)
    target_max, logit_max = lax.pmax((target_top, logit_top), "vocab")
    target_sum, logit_sum = lax.psum(
        (
            jnp.sum(jnp.exp(target_logits - target_max[:, None]), axis=1),
            jnp.sum(jnp.exp(logits - logit_max[:, None]), axis=1),
        ),
        "vocab",
    )
    target_lse = target_max + jnp.log(target_sum)
    logit_lse = logit_max + jnp.log(logit_sum)
    target = jnp.exp(target_logits - target_lse[:, None])
    predicted = jnp.exp(logits - logit_lse[:, None])
    local_term = (
        jnp.sum(target * (target_logits - logits)) + jnp.sum(logit_lse - target_lse) / vocab_groups
    )
    divergence = lax.psum(local_term, ("vocab", "dp")) / token_count
    grad_logits = (predicted - target).astype(jnp.bfloat16)
    grad_part = lax.dot_general(
        lax.all_gather(grad_logits, "dp", axis=0, tiled=True),
        head,
        (((1,), (1,)), ((), ())),
        preferred_element_type=jnp.float32,
    )
    grad_normed = lax.psum(grad_part, "vocab")
    grad_scaled = grad_normed * gain
    inner = lax.psum(jnp.sum(grad_scaled * scaled, axis=1), "dp") / model_width
    grad_projected = (inverse[:, None] * (grad_scaled - scaled * inner[:, None])).astype(
        jnp.bfloat16
    )
    grad_weights = lax.dot_general(
        features, grad_projected, (((0,), (0,)), ((), ())), preferred_element_type=jnp.float32
    )
    grad_offsets = jnp.sum(grad_projected.astype(jnp.float32), axis=0)
    return (grad_weights[None], grad_offsets[None], jnp.reshape(divergence, (1,)))


def solution(mesh):
    in_specs = (
        P("layer", None, "vocab"),
        P("layer", "vocab", "dp"),
        P("layer", "dp"),
        P("dp"),
        P("dp", "vocab"),
        P("dp", "layer", "vocab"),
    )
    out_specs = (P("layer", "vocab", "dp"), P("layer", "dp"), P("layer"))
    return jax.shard_map(shards, mesh=mesh, in_specs=in_specs, out_specs=out_specs, check_vma=False)
```

profile of v0, /device:TPU:1, one launch (start us, length us, event | category | flops | bytes accessed | tf_op | source)
XLA Modules:
  0.0 691.9 jit_solution(17128691850196258132)
XLA Ops:
  8.0 0.0 copy-start
  8.0 0.0 copy-start.3
  8.0 0.0 all-reduce.4.cloned.1.call-start
  8.1 1.0 copy-done
  9.0 2.7 fusion.11
  11.7 0.0 copy-start.4
  11.7 0.0 all-reduce.4.cloned.1.call-update
  11.8 0.0 all-gather.3.cloned.1.call-start
  11.8 0.5 all-gather.3.cloned.1.call-update
  12.3 0.0 reduce-scatter.2.cloned.1.call-start
  12.4 102.9 %all-reduce.4.cloned.1.call-done = f32[512,1024]{1,0:T(8,128)} async-done(((f32[512,1024]{1,0:T(8,128)}), f32[512,1024]{1,0:T(8,128)}) %all-reduce.4.cloned.1.call-update) | async-done | bytes 2097168 | tf_op jit(solution)/shard_map/psum | solution.py:21
  115.3 0.0 copy-start.1
  115.3 0.0 copy-done.3
  115.3 2.0 multiply_reduce_fusion.1
  117.3 10.9 %psum.50 = f32[512]{0:T(512)S(1)} all-reduce(f32[512]{0:T(512)S(1)} %multiply_reduce_fusion.1), channel_id=1, replica_groups=mesh['layer'=4,'vocab'=16,'dp'=4] {'dp'}, use_global_device_ids=true, to_apply=%region_2.0 | all-reduce | flops 512 | bytes 4096 | tf_op jit(solution)/shard_map/psum | solution.py:23
  128.2 0.0 copy-done.4
  128.2 0.0 copy-done.1
  128.2 10.3 %fusion.7 = f32[512,4096]{1,0:T(8,128)} fusion(bf16[1024,4096]{1,0:T(8,128)(2,1)} %param.10, f32[512,1024]{1,0:T(8,128)S(1)} %copy-done.1, f32[1024]{0:T(1024)S(1)} %copy-done.4, f32[512]{0:T(512)S(1)} %add_rsqrt_fusion, f32[1024]{0:T(1024)S(1)} %bitcast.25), kind=kOutput, calls=%fused_computation.18 | convolution fusion | flops 4297064448 | bytes 18884608 | tf_op jit(solution)/shard_map/dot_general | solution.py:28
  138.5 0.0 reduce-scatter.2.cloned.1.call-update
  138.5 0.0 all-gather.5.cloned.1.call-start
  138.6 0.0 all-gather.3.cloned.1.call-done
  138.6 1.4 reduce_max.24
  140.1 130.3 %reduce-scatter.2.cloned.1.call-done = f32[128,4096]{1,0:T(8,128)} async-done(((f32[512,4096]{1,0:T(8,128)}), f32[128,4096]{1,0:T(8,128)}) %reduce-scatter.2.cloned.1.call-update) | async-done | bytes 2097168 | tf_op jit(solution)/shard_map/reduce_scatter | solution.py:27
  270.3 1.8 reduce_max.23
  272.1 33.6 %all-reduce = (f32[128]{0:T(128)S(1)}, f32[128]{0:T(128)S(1)}) all-reduce(bf16[128]{0:T(256)(128)(2,1)S(1)} %reduce_max.24, f32[128]{0:T(128)S(1)} %reduce_max.23), channel_id=1, replica_groups=mesh['layer'=4,'vocab'=16,'dp'=4] {'vocab'}, use_global_device_ids=true, to_apply=%region_9.0 | all-reduce | flops 256 | bytes 1792 | tf_op jit(solution)/shard_map/pmax | solution.py:35
  305.7 1.7 fusion.1
  307.4 28.5 %psum.52 = f32[128]{0:T(128)S(1)} all-reduce(f32[128]{0:T(128)S(1)} %fusion.1), channel_id=1, replica_groups=mesh['layer'=4,'vocab'=16,'dp'=4] {'vocab'}, use_global_device_ids=true, to_apply=%region_11.0 | all-reduce | flops 128 | bytes 1024 | tf_op jit(solution)/shard_map/psum | solution.py:36
  335.9 3.4 fusion.6
  339.3 30.4 %psum.51 = f32[128]{0:T(128)S(1)} all-reduce(f32[128]{0:T(128)S(1)} %get-tuple-element.7), channel_id=1, replica_groups=mesh['layer'=4,'vocab'=16,'dp'=4] {'vocab'}, use_global_device_ids=true, to_apply=%region_7.0 | all-reduce | flops 128 | bytes 1024 | tf_op jit(solution)/shard_map/psum | solution.py:36
  369.7 0.6 subtract_reduce_fusion
  370.3 3.5 fusion.5
  373.8 0.0 all-gather.5.cloned.1.call-update
  373.8 0.0 all-reduce.6.cloned.1.call-start
  373.9 79.1 %all-gather.5.cloned.1.call-done = bf16[512,4096]{1,0:T(8,128)(2,1)} async-done(((bf16[128,4096]{1,0:T(8,128)(2,1)}), bf16[512,4096]{1,0:T(8,128)(2,1)}) %all-gather.5.cloned.1.call-update) | async-done | bytes 4194320 | tf_op jit(solution)/shard_map/all_gather | solution.py:53
  453.0 10.5 %fusion.15 = f32[512,1024]{1,0:T(8,128)} fusion(bf16[512,4096]{1,0:T(8,128)(2,1)} %all-gather.5.cloned.1.call-done, bf16[1024,4096]{1,0:T(8,128)(2,1)} %param.10), kind=kOutput, calls=%fused_computation.31 | convolution fusion | flops 4294967296 | bytes 14680064 | tf_op jit(solution)/shard_map/dot_general | solution.py:52
  463.5 0.0 all-reduce.6.cloned.1.call-update
  464.8 201.5 %psum.55 = f32[]{:T(128)} all-reduce(f32[]{:T(128)S(6)} %add.48), channel_id=1, replica_groups=mesh['layer'=4,'vocab'=16,'dp'=4] {'vocab','dp'}, use_global_device_ids=true, to_apply=%region_18.0 | all-reduce | flops 1 | bytes 8 | tf_op jit(solution)/shard_map/psum | solution.py:50
  667.0 0.0 all-reduce.6.cloned.1.call-done
  667.0 2.1 multiply_reduce_fusion
  669.1 9.8 %psum.54 = f32[512]{0:T(512)S(1)} all-reduce(f32[512]{0:T(512)S(1)} %multiply_reduce_fusion), channel_id=1, replica_groups=mesh['layer'=4,'vocab'=16,'dp'=4] {'dp'}, use_global_device_ids=true, to_apply=%region_14.0 | all-reduce | flops 512 | bytes 4096 | tf_op jit(solution)/shard_map/psum | solution.py:60
  679.0 0.0 copy-start.2
  679.0 2.9 convert_reduce_fusion
  681.9 0.0 copy-done.2
  681.9 0.5 convolution_bitcast_fusion
  682.3 1.3 copy.9
  (3 shorter events, 0.0 us)
Async XLA Ops:
  8.0 1.0 copy-start
  8.0 107.3 %copy-start.3 = (f32[1,1024]{1,0:T(1,128)S(1)}, f32[1,1024]{1,0:T(1,128)}, u32[]{:S(2)}) copy-start(f32[1,1024]{1,0:T(1,128)} %param.8) | copy-start | bytes 12292
  8.0 107.3 %all-reduce.4.cloned.1.call-start = ((), (), s32[]{:S(2)}) async-start(), calls=%async_computation.1 | async-start | bytes 4194304 | tf_op jit(solution)/shard_map/psum | solution.py:21
  11.7 116.5 %copy-start.4 = (f32[1024]{0:T(1024)S(1)}, f32[1024]{0:T(1024)}, u32[]{:S(2)}) copy-start(f32[1024]{0:T(1024)} %param.9) | copy-start | bytes 12292
  11.8 126.8 %all-gather.3.cloned.1.call-start = ((), (), s32[]{:S(2)}) async-start(), calls=%async_computation.3 | async-start | bytes 1310720 | tf_op jit(solution)/shard_map/all_gather | solution.py:19
  12.3 258.0 %reduce-scatter.2.cloned.1.call-start = ((), (), s32[]{:S(2)}) async-start(), calls=%async_computation.2 | async-start | bytes 10485760 | tf_op jit(solution)/shard_map/reduce_scatter | solution.py:27
  115.3 13.0 %copy-start.1 = (f32[512,1024]{1,0:T(8,128)S(1)}, f32[512,1024]{1,0:T(8,128)}, u32[]{:S(2)}) copy-start(f32[512,1024]{1,0:T(8,128)} %all-reduce.4.cloned.1.call-done) | copy-start | bytes 6291460
  138.5 314.4 %all-gather.5.cloned.1.call-start = ((), (), s32[]{:S(2)}) async-start(), calls=%async_computation.4 | async-start | bytes 5242880 | tf_op jit(solution)/shard_map/all_gather | solution.py:53
  373.8 293.1 %all-reduce.6.cloned.1.call-start = ((), (), s32[]{:S(2)}) async-start(), calls=%async_computation.5 | async-start | bytes 4194304 | tf_op jit(solution)/shard_map/psum | solution.py:58
  679.0 2.9 copy-start.2
Sparse Core Ops, SparseCore 0:
  12.2 103.0 all-reduce.3
  138.6 131.6 reduce-scatter.1
  374.0 78.9 all-gather.4
  463.6 95.0 all-reduce.5
Sparse Core Ops, SparseCore 1:
  14.0 36.5 all-gather.2
where the time goes:
time: 695 us; the launch traced here: 692 us
  blocking collectives  315 us (45%)
  waiting for transfers between devices  313 us (45%)
  matrix products  23.9 us (3%)
  other arithmetic  19.4 us (3%)
  between operations  18.3 us (3%)
    psum x1, blocking collectives, shards(): divergence = lax.psum(local_term, ('vocab', 'dp')) / token_count  202 us
    reduce_scatter x1, waiting for transfers between devices, shards(): lax.psum_scatter(jnp.dot(normed_here, head, preferred_element_type=jnp.fl...  130 us
    psum x1, waiting for transfers between devices, shards(): lax.psum(jnp.dot(features, weights, preferred_element_type=jnp.float32),...  103 us
    all_gather x1, waiting for transfers between devices, shards(): lax.all_gather(grad_logits, 'dp', axis=0, tiled=True)  79.1 us
    psum x2, blocking collectives, shards(): lax.psum((jnp.sum(jnp.exp(target_logits - target_max[:, None]), axis=1),...  58.9 us
    pmax x1, blocking collectives, shards(): target_max, logit_max = lax.pmax((target_top, logit_top), 'vocab')  33.6 us
  transfers between devices with their start and end apart: 5, of which 3 were waited for; matrix products, arithmetic and copies ran while one was open for 2% of the time, Pallas kernels for 0%

commit v1 on v0

v1 whole, which is shorter than its diff:
```python
import jax
import jax.numpy as jnp
from jax import lax
from jax.experimental import pallas as pl
from jax.experimental.pallas import tpu as pltpu
from jax.sharding import PartitionSpec as P

D = 4096
TOKENS = 512
LAYERS = 4
GROUPS = 16
BLOCKS = 4
BLOCK = D // BLOCKS
QUARTER = 1024
ROWS = TOKENS // GROUPS
HALF = BLOCK // 2
CHUNK = 32
CHUNKS = HALF // CHUNK

epsilon = 1e-05
f32 = jnp.float32
bf16 = jnp.bfloat16
MESH = pl.DeviceIdType.MESH


def aligned(start, size, unit=None):
    return pl.ds(pl.multiple_of(start, unit or size), size)


def kernel(
    hidden, translator, bias, gain, head, final, grad_out, div_out,
    heads, passing, normed, partial, parts, target, scaled, squares, logits, stats, stats2, ends_lse,
    grads, crossing, crossed, summing, sums, half_sum, other_sum, inners, finals,
    chain_send, chain_recv, pass_send, pass_recv, head_send, head_recv, fin_send, fin_recv,
    rs_send, rs_recv, sq_send, sq_recv, ag_send, ag_recv, opp_send, opp_recv, sib_send, sib_recv,
    st_send, st_recv, st2_send, st2_recv, gx_send, gx_recv, gs_send, gs_recv, go_send, go_recv,
    in_send, in_recv, gp_send, gp_recv, local_sem,
):
    l = lax.axis_index("layer")
    v = lax.axis_index("vocab")
    d = lax.axis_index("dp")
    h = lax.div(d, 2)
    c = lax.rem(d, 2)
    sib = h * 2 + 1 - c
    opp = lax.rem(d + 2, BLOCKS)
    opp_sib = (1 - h) * 2 + 1 - c
    up_l = lax.rem(l + 1, LAYERS)
    up_d = lax.rem(d + 2 * lax.div(l + 1, LAYERS), BLOCKS)
    down_l = lax.rem(l + LAYERS - 1, LAYERS)
    down_d = lax.rem(d + 2 * (1 - lax.div(l + LAYERS - 1, LAYERS)), BLOCKS)
    column = l * BLOCKS + d
    NCOL = LAYERS * BLOCKS

    def in_plane(k):
        return lax.rem(v + k, GROUPS)

    def in_column(k):
        return lax.rem(column + k, NCOL)

    def remote(src, dst, send, recv, ll, vv, dd):
        return pltpu.make_async_remote_copy(
            src_ref=src, dst_ref=dst, send_sem=send, recv_sem=recv,
            device_id=(ll, vv, dd), device_id_type=MESH,
        )

    def arrive(dst, sem):
        remote(dst, dst, sem, sem, l, v, d).wait_recv()

    def sent(src, sem):
        remote(src, src, sem, sem, l, v, d).wait_send()

    def each(lo, hi, f):
        def step(k, carry):
            f(k)
            return carry
        lax.fori_loop(lo, hi, step, 0)

    barrier = pltpu.get_barrier_semaphore()

    def greet_plane(k):
        pl.semaphore_signal(barrier, inc=1, device_id=(l, in_plane(k), d), device_id_type=MESH)

    def greet_column(k):
        m = in_column(k)
        pl.semaphore_signal(
            barrier, inc=1, device_id=(lax.div(m, BLOCKS), v, lax.rem(m, BLOCKS)), device_id_type=MESH
        )

    each(1, GROUPS, greet_plane)
    each(1, NCOL, greet_column)
    pl.semaphore_wait(barrier, GROUPS - 1 + NCOL - 1)

    def cols(q):
        return aligned(q * QUARTER, QUARTER)

    def rows_of(s, k):
        return aligned(s * HALF + k * CHUNK, CHUNK)

    def chain_copy(s, j, k, from_own):
        rows = rows_of(s, k)
        ll, dd = (up_l, up_d) if s == 0 else (down_l, down_d)
        if from_own:
            src = head.at[rows, cols((1 - h) * 2 + (c if j == 0 else 1 - c))]
            dst = heads.at[d, rows, :] if j == 0 else passing.at[rows, :]
        else:
            src = heads.at[opp, rows, :] if j == 0 else passing.at[rows, :]
            dst = src
        return remote(src, dst, chain_send.at[s, j, k], chain_recv.at[s, j, k], ll, v, dd)

    ends = (l == LAYERS - 1, l == 0)
    relays = (l != LAYERS - 1, l != 0)

    def source(s):
        def one(k):
            chain_copy(s, 0, k, True).start()
            chain_copy(s, 1, k, True).start()

        @pl.when(ends[s])
        def _():
            each(0, CHUNKS, one)

    def chain(lo, hi):
        def one(k):
            for s in (0, 1):
                rows = rows_of(s, k)
                arrive(heads.at[opp, rows, :], chain_recv.at[s, 0, k])
                arrive(passing.at[rows, :], chain_recv.at[s, 1, k])

                @pl.when(relays[s])
                def _(s=s):
                    chain_copy(s, 0, k, False).start()
                    chain_copy(s, 1, k, False).start()

                remote(
                    passing.at[rows, :], heads.at[opp, rows, :],
                    pass_send.at[s, k], pass_recv.at[s, k], l, v, sib,
                ).start()

        each(lo, hi, one)

    source(0)
    source(1)
    head_copy = remote(head.at[:, cols(sib)], heads.at[d], head_send, head_recv, l, v, sib)
    head_copy.start()
    own_head = pltpu.make_async_copy(head.at[:, cols(d)], heads.at[d], local_sem.at[0])
    own_head.start()
    own_final = pltpu.make_async_copy(
        final.at[:, cols(d)], target.at[aligned(d * 128 + l * 32, 32), :], local_sem.at[1]
    )
    own_final.start()

    def product(n):
        at = aligned(n * 256, 256)
        partial[:, at] = jnp.dot(hidden[...], translator[:, at], preferred_element_type=f32)

    each(0, BLOCK // 256, product)

    def own_rows(p):
        return aligned(p * ROWS, ROWS)

    def scatter(k):
        p = in_plane(k)
        remote(partial.at[own_rows(p), :], parts.at[v], rs_send.at[k], rs_recv.at[v], l, p, d).start()

    each(1, GROUPS, scatter)

    def final_copy(k):
        m = in_column(k)
        ll, dd = lax.div(m, BLOCKS), lax.rem(m, BLOCKS)
        remote(
            final.at[:, cols(dd)], target.at[aligned(d * 128 + l * 32, 32), :],
            fin_send.at[k], fin_recv.at[column], ll, v, dd,
        ).start()

    each(1, NCOL, final_copy)

    scaled[...] = partial[own_rows(v), :] + bias[...]

    def add_part(k):
        p = in_plane(k)
        arrive(parts.at[p], rs_recv.at[p])
        scaled[...] += parts[p]

    each(1, GROUPS, add_part)
    projected = scaled[...]
    squares[d] = jnp.broadcast_to(jnp.sum(projected * projected, axis=1, keepdims=True), (ROWS, 128))

    def to_blocks(buf, send, recv):
        def go(k):
            dd = lax.rem(d + k, BLOCKS)
            remote(buf.at[d], buf.at[d], send.at[k], recv.at[d], l, v, dd).start()
        each(1, BLOCKS, go)

    def from_blocks(buf, recv):
        def come(k):
            dd = lax.rem(d + k, BLOCKS)
            arrive(buf.at[dd], recv.at[dd])
        each(1, BLOCKS, come)

    to_blocks(squares, sq_send, sq_recv)
    chain(0, 4)
    from_blocks(squares, sq_recv)
    inverse = lax.rsqrt(jnp.sum(squares[...], axis=0)[:, :1] / D + epsilon)
    scaled[...] = projected * inverse
    normed[d, own_rows(v), :] = (scaled[...] * gain[...]).astype(bf16)

    mine = normed.at[d, own_rows(v), :]
    opp_copy = remote(mine, mine, opp_send, opp_recv, l, v, opp)
    opp_copy.start()

    def gather(block, i):
        def go(k):
            ref = normed.at[block, own_rows(v), :]
            remote(ref, ref, ag_send.at[i, k], ag_recv.at[i, v], l, in_plane(k), d).start()
        each(1, GROUPS, go)

    def gathered(block, i):
        def come(k):
            p = in_plane(k)
            arrive(normed.at[block, own_rows(p), :], ag_recv.at[i, p])
        each(1, GROUPS, come)

    gather(d, 0)
    chain(4, 6)
    arrive(normed.at[opp, own_rows(v), :], opp_recv)
    gather(opp, 1)
    chain(6, 8)
    gathered(d, 0)
    sib_copy0 = remote(normed.at[d], normed.at[d], sib_send.at[0], sib_recv.at[0], l, v, sib)
    sib_copy0.start()
    chain(8, 10)
    gathered(opp, 1)
    sib_copy1 = remote(normed.at[opp], normed.at[opp], sib_send.at[1], sib_recv.at[1], l, v, sib)
    sib_copy1.start()
    own_head.wait()
    own_final.wait()

    def multiply(block, first):
        def go(n):
            at = aligned(n * 256, 256)
            value = jnp.dot(normed[block], heads[block, :, at], preferred_element_type=f32)
            if first:
                logits[:, at] = value
            else:
                logits[:, at] += value
        each(0, QUARTER // 256, go)

    multiply(d, True)
    chain(10, 13)
    arrive(normed.at[sib], sib_recv.at[0])
    arrive(heads.at[sib], head_recv)
    multiply(sib, False)
    chain(13, CHUNKS)
    multiply(opp, False)
    arrive(normed.at[opp_sib], sib_recv.at[1])

    def passed(k):
        for s in (0, 1):
            arrive(heads.at[opp_sib, rows_of(s, k), :], pass_recv.at[s, k])

    each(0, CHUNKS, passed)
    multiply(opp_sib, False)

    def final_arrived(k):
        m = in_column(k)
        ll, dd = lax.div(m, BLOCKS), lax.rem(m, BLOCKS)
        arrive(target.at[aligned(dd * 128 + ll * 32, 32), :], fin_recv.at[m])

    each(1, NCOL, final_arrived)

    def local_stats(t):
        at = aligned(t * 128, 128)
        want = target[at, :].astype(f32)
        have = logits[at, :]
        want_top = jnp.max(want, axis=1, keepdims=True)
        want_exp = jnp.exp(want - want_top)
        have_top = jnp.max(have, axis=1, keepdims=True)
        have_sum = jnp.sum(jnp.exp(have - have_top), axis=1, keepdims=True)
        want_sum = jnp.sum(want_exp, axis=1, keepdims=True)
        cross = jnp.sum(want_exp * (want - have), axis=1, keepdims=True)
        lane = lax.broadcasted_iota(jnp.int32, (128, 128), 1)
        packed = jnp.where(
            lane == 0, want_top,
            jnp.where(
                lane == 1, want_sum,
                jnp.where(lane == 2, cross, jnp.where(lane == 3, have_top, have_sum)),
            ),
        )
        stats[v, :, at] = packed.T[0:8, :]

    each(0, TOKENS // 128, local_stats)

    def stats_out(k):
        remote(stats.at[v], stats.at[v], st_send.at[k], st_recv.at[v], l, in_plane(k), d).start()

    def stats_in(k):
        p = in_plane(k)
        arrive(stats.at[p], st_recv.at[p])

    each(1, GROUPS, stats_out)
    each(1, GROUPS, stats_in)

    def merge(buf):
        want_top = jnp.max(buf[:, 0, :], axis=0, keepdims=True)
        have_top = jnp.max(buf[:, 3, :], axis=0, keepdims=True)
        want_scale = jnp.exp(buf[:, 0, :] - want_top)
        have_scale = jnp.exp(buf[:, 3, :] - have_top)
        want_sum = jnp.sum(buf[:, 1, :] * want_scale, axis=0, keepdims=True)
        cross = jnp.sum(buf[:, 2, :] * want_scale, axis=0, keepdims=True)
        have_sum = jnp.sum(buf[:, 4, :] * have_scale, axis=0, keepdims=True)
        return want_top, want_sum, cross, have_top, have_sum

    merged = merge(stats)
    stats2[d] = jnp.concatenate(merged + merged[2:], axis=0)
    to_blocks(stats2, st2_send, st2_recv)
    from_blocks(stats2, st2_recv)
    want_top, want_sum, cross, have_top, have_sum = merge(stats2)
    want_lse = want_top + jnp.log(want_sum)
    have_lse = have_top + jnp.log(have_sum)
    per_token = cross / want_sum + (have_lse - want_lse)
    div_out[...] = jnp.broadcast_to(jnp.sum(per_token, axis=1, keepdims=True) / TOKENS, (8, 128))
    ends_lse[0:1, :] = want_lse
    ends_lse[1:2, :] = have_lse
    ends_lse[2:8, :] = jnp.zeros((6, TOKENS), f32)

    def grad_rows(t):
        at = aligned(t * 128, 128)
        both = jnp.concatenate([ends_lse[:, at]] * 16, axis=0).T
        want = jnp.exp(target[at, :].astype(f32) - both[:, 0:1])
        have = jnp.exp(logits[at, :] - both[:, 1:2])
        grads[at, :] = (have - want).astype(bf16)

    each(0, TOKENS // 128, grad_rows)

    def back(block, write):
        def go(n):
            at = aligned(n * 256, 256)
            write(
                at,
                lax.dot_general(
                    grads[...], heads[block, at, :], (((1,), (1,)), ((), ())),
                    preferred_element_type=f32,
                ),
            )
        each(0, BLOCK // 256, go)

    def crossing_copy(i):
        return remote(crossing.at[i], crossed.at[i], gx_send.at[i], gx_recv.at[i], l, v, sib)

    for i, block in ((0, opp_sib), (1, sib)):
        def to_crossing(at, value, i=i):
            crossing[i, :, at] = value.astype(bf16)
        back(block, to_crossing)
        crossing_copy(i).start()

    for i, block in ((0, opp), (1, d)):
        def to_logits(at, value):
            logits[:, at] = value
        back(block, to_logits)
        arrive(crossed.at[i], gx_recv.at[i])

        def add_rows(t, i=i):
            at = aligned(t * 128, 128)
            summing[i, at, :] = (logits[at, :] + crossed[i, at, :].astype(f32)).astype(bf16)
        each(0, TOKENS // 128, add_rows)

        def scatter_sum(k, i=i):
            p = in_plane(k)
            remote(
                summing.at[i, own_rows(p), :], sums.at[i, v],
                gs_send.at[i, k], gs_recv.at[i, v], l, p, d,
            ).start()
        each(1, GROUPS, scatter_sum)

    for i, out in ((0, half_sum), (1, inners)):
        if i == 0:
            out[...] = summing[0, own_rows(v), :].astype(f32)
        else:
            finals[...] = summing[1, own_rows(v), :].astype(f32)

        def add_sum(k, i=i):
            p = in_plane(k)
            arrive(sums.at[i, p], gs_recv.at[i, p])
            if i == 0:
                half_sum[...] += sums[0, p].astype(f32)
            else:
                finals[...] += sums[1, p].astype(f32)
        each(1, GROUPS, add_sum)
        if i == 0:
            go_copy = remote(half_sum, other_sum, go_send, go_recv, l, v, opp)
            go_copy.start()

    arrive(other_sum, go_recv)
    grad_scaled = (finals[...] + other_sum[...]) * gain[...]
    inners[d] = jnp.broadcast_to(
        jnp.sum(grad_scaled * scaled[...], axis=1, keepdims=True), (ROWS, 128)
    )
    to_blocks(inners, in_send, in_recv)
    from_blocks(inners, in_recv)
    inner = jnp.sum(inners[...], axis=0)[:, :1] / D
    inverse = lax.rsqrt(jnp.sum(squares[...], axis=0)[:, :1] / D + epsilon)
    grad_out[own_rows(v), :] = (inverse * (grad_scaled - scaled[...] * inner)).astype(bf16)

    def grad_go(k):
        ref = grad_out.at[own_rows(v), :]
        remote(ref, ref, gp_send.at[k], gp_recv.at[v], l, in_plane(k), d).start()

    def grad_come(k):
        p = in_plane(k)
        arrive(grad_out.at[own_rows(p), :], gp_recv.at[p])

    each(1, GROUPS, grad_go)
    each(1, GROUPS, grad_come)

    for s in (0, 1):
        def chain_sent(k, s=s):
            chain_copy(s, 0, k, False).wait_send()
            chain_copy(s, 1, k, False).wait_send()
            sent(passing.at[rows_of(s, k), :], pass_send.at[s, k])
        each(0, CHUNKS, chain_sent)
    head_copy.wait_send()
    opp_copy.wait_send()
    sib_copy0.wait_send()
    sib_copy1.wait_send()
    go_copy.wait_send()
    crossing_copy(0).wait_send()
    crossing_copy(1).wait_send()

    def plane_sent(k):
        sent(parts.at[0], rs_send.at[k])
        sent(mine, ag_send.at[0, k])
        sent(mine, ag_send.at[1, k])
        sent(stats.at[0], st_send.at[k])
        sent(sums.at[0, 0], gs_send.at[0, k])
        sent(sums.at[0, 0], gs_send.at[1, k])
        sent(grad_out.at[own_rows(v), :], gp_send.at[k])
        sent(target.at[aligned(d * 128 + l * 32, 32), :], fin_send.at[k])

    each(1, GROUPS, plane_sent)

    def blocks_sent(k):
        sent(squares.at[0], sq_send.at[k])
        sent(stats2.at[0], st2_send.at[k])
        sent(inners.at[0], in_send.at[k])

    each(1, BLOCKS, blocks_sent)


def run(hidden, translator, bias, gain, head, final):
    dma = pltpu.SemaphoreType.DMA
    vmem = pltpu.VMEM
    in_vmem = pl.BlockSpec(memory_space=pltpu.VMEM)
    anywhere = pl.BlockSpec(memory_space=pl.ANY)
    return pl.pallas_call(
        kernel,
        out_shape=[
            jax.ShapeDtypeStruct((TOKENS, BLOCK), bf16),
            jax.ShapeDtypeStruct((8, 128), f32),
        ],
        in_specs=[in_vmem] * 4 + [anywhere] * 2,
        out_specs=[in_vmem] * 2,
        scratch_shapes=[
            vmem((BLOCKS, BLOCK, QUARTER), bf16),
            vmem((BLOCK, QUARTER), bf16),
            vmem((BLOCKS, TOKENS, BLOCK), bf16),
            vmem((TOKENS, BLOCK), f32),
            vmem((GROUPS, ROWS, BLOCK), f32),
            vmem((TOKENS, QUARTER), bf16),
            vmem((ROWS, BLOCK), f32),
            vmem((BLOCKS, ROWS, 128), f32),
            vmem((TOKENS, QUARTER), f32),
            vmem((GROUPS, 8, TOKENS), f32),
            vmem((BLOCKS, 8, TOKENS), f32),
            vmem((8, TOKENS), f32),
            vmem((TOKENS, QUARTER), bf16),
            vmem((2, TOKENS, BLOCK), bf16),
            vmem((2, TOKENS, BLOCK), bf16),
            vmem((2, TOKENS, BLOCK), bf16),
            vmem((2, GROUPS, ROWS, BLOCK), bf16),
            vmem((ROWS, BLOCK), f32),
            vmem((ROWS, BLOCK), f32),
            vmem((BLOCKS, ROWS, 128), f32),
            vmem((ROWS, BLOCK), f32),
            dma((2, 2, CHUNKS)), dma((2, 2, CHUNKS)),
            dma((2, CHUNKS)), dma((2, CHUNKS)),
            dma, dma,
            dma((16,)), dma((16,)),
            dma((GROUPS,)), dma((GROUPS,)),
            dma((BLOCKS,)), dma((BLOCKS,)),
            dma((2, GROUPS)), dma((2, GROUPS)),
            dma, dma,
            dma((2,)), dma((2,)),
            dma((GROUPS,)), dma((GROUPS,)),
            dma((BLOCKS,)), dma((BLOCKS,)),
            dma((2,)), dma((2,)),
            dma((2, GROUPS)), dma((2, GROUPS)),
            dma, dma,
            dma((BLOCKS,)), dma((BLOCKS,)),
            dma((GROUPS,)), dma((GROUPS,)),
            dma((2,)),
        ],
        compiler_params=pltpu.CompilerParams(
            collective_id=0, has_side_effects=True, vmem_limit_bytes=56 * 1024 * 1024
        ),
        name="lens",
    )(hidden, translator, bias, gain, head, final)


def shards(hidden, translator, bias, gain, head, final_logits):
    features = hidden[0]
    grad_projected, divergence = run(
        features, translator[0], bias, gain[None], head, final_logits[0]
    )
    grad_weights = lax.dot_general(
        features, grad_projected, (((0,), (0,)), ((), ())), preferred_element_type=f32
    )
    grad_offsets = jnp.sum(grad_projected.astype(f32), axis=0)
    return (grad_weights[None], grad_offsets[None], divergence[0, :1])


def solution(mesh):
    in_specs = (
        P("layer", None, "vocab"),
        P("layer", "vocab", "dp"),
        P("layer", "dp"),
        P("dp"),
        P("dp", "vocab"),
        P("dp", "layer", "vocab"),
    )
    out_specs = (P("layer", "vocab", "dp"), P("layer", "dp"), P("layer"))
    return jax.shard_map(shards, mesh=mesh, in_specs=in_specs, out_specs=out_specs, check_vma=False)
```

time: 695 us -> 528 us (0.76)
  Pallas kernels: 0 us -> 521 us
  blocking collectives: 315 us -> 0 us
  waiting for transfers between devices: 313 us -> 0 us
  matrix products: 23.9 us -> 1.69 us
  between operations: 18.3 us -> 0.66 us
  other arithmetic: 19.4 us -> 2 us
    pallas_call x0 -> x1, Pallas kernels: none -> 521 us  [run(): pl.pallas_call(kernel, out_shape=[jax.ShapeDtypeStruct((TOKENS, BLOCK), b...]
    psum x5 -> x0, blocking collectives: 281 us -> none  [the longest x1 202 us: shards(): divergence = lax.psum(local_term, ('vocab', 'dp')) / token_count]
    reduce_scatter x1 -> x0, waiting for transfers between devices: 130 us -> none  [shards(): lax.psum_scatter(jnp.dot(normed_here, head, preferred_element_type=jnp.fl...]
    psum x2 -> x0, waiting for transfers between devices: 103 us -> none  [the longest x1 103 us: shards(): lax.psum(jnp.dot(features, weights, preferred_element_type=jnp.float32),...]
    all_gather x2 -> x0, waiting for transfers between devices: 79.1 us -> none  [the longest x1 79.1 us: shards(): lax.all_gather(grad_logits, 'dp', axis=0, tiled=True)]
    pmax x1 -> x0, blocking collectives: 33.6 us -> none  [shards(): target_max, logit_max = lax.pmax((target_top, logit_top), 'vocab')]
    dot_general x3 -> x0, matrix products: 23.5 us -> none  [the longest x1 10.5 us: shards(): lax.dot_general(lax.all_gather(grad_logits, 'dp', axis=0, tiled=True), he...]
    reduce_sum x6 -> x1, other arithmetic: 12.7 us -> 2 us  [shards(): grad_offsets = jnp.sum(grad_projected.astype(f32), axis=0)]
  transfers between devices with their start and end apart: 5 -> 0, of which waited for: 3 -> 0; matrix products, arithmetic and copies ran while one was open for 2% -> 0% of each run, Pallas kernels for 0% -> 0%
where the time goes in v1:
time: 528 us
  Pallas kernels  521 us (99%)
    pallas_call x1, Pallas kernels, run(): pl.pallas_call(kernel, out_shape=[jax.ShapeDtypeStruct((TOKENS, BLOCK), b...  521 us

profile of v1, /device:TPU:1, one launch (start us, length us, event | category | flops | bytes accessed | tf_op | source)
XLA Modules:
  0.0 528.0 jit_solution(3934033432654853090)
XLA Ops:
  0.6 0.0 copy-start
  0.6 521.2 %lens.1 = (bf16[512,1024]{1,0:T(8,128)(2,1)}, f32[8,128]{1,0:T(8,128)}) custom-call(bf16[512,256]{1,0:T(8,128)(2,1)} %bitcast.13, bf16[256,1024]{1,0:T(8,128)(2,1)} %bitcast.14, f32[1,1024]{1,0:T(1,128)} %bias.1, f32[1,1024]{1,0:T(1,128)} %bitcast.16, bf16[1024,4096]{1,0:T(8,128)(2,1)} %head.1, bf16[32,4096]{1,0:T(8,128)(2,1)} %bitcast.15), custom_call_target="tpu_custom_call" | custom-call | tf_op jit(solution)/shard_map/lens/pallas_call | solution.py:454
  521.9 1.2 slice.3
  523.0 2.0 convert_reduce_fusion
  525.0 0.0 copy-done
  525.0 1.7 convolution_bitcast_fusion
  526.7 1.3 copy.9
Async XLA Ops:
  0.6 524.4 %copy-start = (bf16[1,512,256]{2,1,0:T(8,128)(2,1)S(1)}, bf16[1,512,256]{2,1,0:T(8,128)(2,1)}, u32[]{:S(2)}) copy-start(bf16[1,512,256]{2,1,0:T(8,128)(2,1)} %param.6) | copy-start | bytes 786436

commit v2 on v1

--- a/solution.py
+++ b/solution.py
@@ -119,22 +119,29 @@
         def _():
             each(0, CHUNKS, one)
 
+    lag = (l, LAYERS - 1 - l)
+    TURNS = CHUNKS + LAYERS - 1
+
     def chain(lo, hi):
-        def one(k):
+        def one(turn):
             for s in (0, 1):
-                rows = rows_of(s, k)
-                arrive(heads.at[opp, rows, :], chain_recv.at[s, 0, k])
-                arrive(passing.at[rows, :], chain_recv.at[s, 1, k])
-
-                @pl.when(relays[s])
-                def _(s=s):
-                    chain_copy(s, 0, k, False).start()
-                    chain_copy(s, 1, k, False).start()
-
-                remote(
-                    passing.at[rows, :], heads.at[opp, rows, :],
-                    pass_send.at[s, k], pass_recv.at[s, k], l, v, sib,
-                ).start()
+                k = turn - lag[s]
+
+                @pl.when(jnp.logical_and(k >= 0, k < CHUNKS))
+                def _(s=s, k=k):
+                    rows = rows_of(s, k)
+                    arrive(heads.at[opp, rows, :], chain_recv.at[s, 0, k])
+                    arrive(passing.at[rows, :], chain_recv.at[s, 1, k])
+
+                    @pl.when(relays[s])
+                    def _():
+                        chain_copy(s, 0, k, False).start()
+                        chain_copy(s, 1, k, False).start()
+
+                    remote(
+                        passing.at[rows, :], heads.at[opp, rows, :],
+                        pass_send.at[s, k], pass_recv.at[s, k], l, v, sib,
+                    ).start()
 
         each(lo, hi, one)
 
@@ -175,6 +182,7 @@
     each(1, NCOL, final_copy)
 
     scaled[...] = partial[own_rows(v), :] + bias[...]
+    chain(0, 6)
 
     def add_part(k):
         p = in_plane(k)
@@ -198,7 +206,7 @@
         each(1, BLOCKS, come)
 
     to_blocks(squares, sq_send, sq_recv)
-    chain(0, 4)
+    chain(6, 8)
     from_blocks(squares, sq_recv)
     inverse = lax.rsqrt(jnp.sum(squares[...], axis=0)[:, :1] / D + epsilon)
     scaled[...] = projected * inverse
@@ -221,14 +229,14 @@
         each(1, GROUPS, come)
 
     gather(d, 0)
-    chain(4, 6)
+    chain(8, 10)
     arrive(normed.at[opp, own_rows(v), :], opp_recv)
     gather(opp, 1)
-    chain(6, 8)
+    chain(10, 12)
     gathered(d, 0)
     sib_copy0 = remote(normed.at[d], normed.at[d], sib_send.at[0], sib_recv.at[0], l, v, sib)
     sib_copy0.start()
-    chain(8, 10)
+    chain(12, 14)
     gathered(opp, 1)
     sib_copy1 = remote(normed.at[opp], normed.at[opp], sib_send.at[1], sib_recv.at[1], l, v, sib)
     sib_copy1.start()
@@ -246,11 +254,11 @@
         each(0, QUARTER // 256, go)
 
     multiply(d, True)
-    chain(10, 13)
+    chain(14, 15)
     arrive(normed.at[sib], sib_recv.at[0])
     arrive(heads.at[sib], head_recv)
     multiply(sib, False)
-    chain(13, CHUNKS)
+    chain(15, TURNS)
     multiply(opp, False)
     arrive(normed.at[opp_sib], sib_recv.at[1])
 

time: 528 us -> 195 us (0.37)
  Pallas kernels: 521 us -> 188 us
    pallas_call x1, Pallas kernels: 521 us -> 188 us  [run(): pl.pallas_call(kernel, out_shape=[jax.ShapeDtypeStruct((TOKENS, BLOCK), b...]
where the time goes in v2:
time: 195 us
  Pallas kernels  188 us (96%)
  local copies, waits for them, and re-layouts  2.5 us (1%)
  other arithmetic  2 us (1%)
    pallas_call x1, Pallas kernels, run(): pl.pallas_call(kernel, out_shape=[jax.ShapeDtypeStruct((TOKENS, BLOCK), b...  188 us

profile of v2, /device:TPU:1, one launch (start us, length us, event | category | flops | bytes accessed | tf_op | source)
XLA Modules:
  0.0 195.1 jit_solution(13481258042961623863)
XLA Ops:
  0.6 0.0 copy-start
  0.6 188.3 %lens.1 = (bf16[512,1024]{1,0:T(8,128)(2,1)}, f32[8,128]{1,0:T(8,128)}) custom-call(bf16[512,256]{1,0:T(8,128)(2,1)} %bitcast.13, bf16[256,1024]{1,0:T(8,128)(2,1)} %bitcast.14, f32[1,1024]{1,0:T(1,128)} %bias.1, f32[1,1024]{1,0:T(1,128)} %bitcast.16, bf16[1024,4096]{1,0:T(8,128)(2,1)} %head.1, bf16[32,4096]{1,0:T(8,128)(2,1)} %bitcast.15), custom_call_target="tpu_custom_call" | custom-call | tf_op jit(solution)/shard_map/lens/pallas_call | solution.py:462
  189.0 1.2 slice.3
  190.1 2.0 %convert_reduce_fusion = f32[1024]{0:T(1024)} fusion(bf16[512,1024]{1,0:T(8,128)(2,1)} %get-tuple-element.5), kind=kLoop, calls=%fused_computation | loop fusion | flops 1047552 | bytes 1052672 | tf_op jit(solution)/shard_map/reduce_sum | solution.py:525
  192.1 0.0 copy-done
  192.1 1.7 convolution_bitcast_fusion
  193.8 1.3 copy.9
Async XLA Ops:
  0.6 191.5 %copy-start = (bf16[1,512,256]{2,1,0:T(8,128)(2,1)S(1)}, bf16[1,512,256]{2,1,0:T(8,128)(2,1)}, u32[]{:S(2)}) copy-start(bf16[1,512,256]{2,1,0:T(8,128)(2,1)} %param.6) | copy-start | bytes 786436

commit v3 on v2

v3 whole, which is shorter than its diff:
```python
import jax
import jax.numpy as jnp
from jax import lax
from jax.experimental import pallas as pl
from jax.experimental.pallas import tpu as pltpu
from jax.sharding import PartitionSpec as P

D = 4096
TOKENS = 512
LAYERS = 4
GROUPS = 16
SIDE = 4
BLOCKS = 4
BLOCK = D // BLOCKS
QUARTER = 1024
ROWS = TOKENS // GROUPS
TILE = 128
HALF = BLOCK // 2
CHUNK = 16
CHUNKS = HALF // CHUNK
LAG = 3

epsilon = 1e-05
f32 = jnp.float32
bf16 = jnp.bfloat16
MESH = pl.DeviceIdType.MESH


def aligned(start, size):
    return pl.ds(pl.multiple_of(start, size), size)


def each(lo, hi, f):
    def step(k, carry):
        f(k)
        return carry

    lax.fori_loop(lo, hi, step, 0)


def kernel(
    hidden, translator, bias, gain, head, final, weights_out, offsets_out, div_out,
    heads, passing, normed, partial, target, final_own, pad, scaled, squares, logits,
    top_stats, want_lse, stats, stats2, lse, cross, inner, crosses, crosses2, grads, crossing, crossed, summing,
    parts, part_mid, part_end, sum_parts, sum_mid, sum_end, half_sum, other_sum, finals, gathered_grad,
    chain_send, chain_recv, pass_send, pass_recv, head_send, head_recv, fin_send, fin_recv,
    sq_send, sq_recv, opp_send, opp_recv, sib_send, sib_recv,
    top_send, top_recv, wl_send, wl_recv, st_send, st_recv, st2_send, st2_recv, cr_send, cr_recv,
    cr2_send, cr2_recv, gx_send, gx_recv, rs_send, rs_recv, ag_send, ag_recv,
    go_send, go_recv, local_sem,
):
    l = lax.axis_index("layer")
    v = lax.axis_index("vocab")
    d = lax.axis_index("dp")
    y = lax.div(v, SIDE)
    x = lax.rem(v, SIDE)
    h = lax.div(d, 2)
    c = lax.rem(d, 2)
    sib = h * 2 + 1 - c
    opp = lax.rem(d + 2, BLOCKS)
    opp_sib = (1 - h) * 2 + 1 - c
    up_l = lax.rem(l + 1, LAYERS)
    up_d = lax.rem(d + 2 * lax.div(l + 1, LAYERS), BLOCKS)
    down_l = lax.rem(l + LAYERS - 1, LAYERS)
    down_d = lax.rem(d + 2 * (1 - lax.div(l + LAYERS - 1, LAYERS)), BLOCKS)
    column = l * BLOCKS + d
    NCOL = LAYERS * BLOCKS

    def in_plane(k):
        return lax.rem(v + k, GROUPS)

    def in_column(k):
        return lax.rem(column + k, NCOL)

    def along_x(k):
        return lax.rem(x + k, SIDE)

    def along_y(k):
        return lax.rem(y + k, SIDE)

    def remote(src, dst, send, recv, ll, vv, dd):
        return pltpu.make_async_remote_copy(
            src_ref=src, dst_ref=dst, send_sem=send, recv_sem=recv,
            device_id=(ll, vv, dd), device_id_type=MESH,
        )

    def arrive(dst, sem):
        remote(dst, dst, sem, sem, l, v, d).wait_recv()

    def sent(src, sem):
        remote(src, src, sem, sem, l, v, d).wait_send()

    leaving = []

    def drain():
        for f in leaving:
            f()

    def start_each(count, make, send, shape):
        each(1, count, lambda k: make(k).start())
        leaving.append(lambda: each(1, count, lambda k: sent(shape, send.at[k])))

    def cols(q):
        return aligned(q * QUARTER, QUARTER)

    def own_rows(p):
        return aligned(p * ROWS, ROWS)

    own_head = pltpu.make_async_copy(head.at[:, cols(d)], heads.at[d], local_sem.at[0])
    own_head.start()
    own_rows_final = aligned(d * TILE + l * ROWS, ROWS)
    own_final = pltpu.make_async_copy(final.at[:, cols(d)], target.at[own_rows_final, :], local_sem.at[1])
    own_final.start()
    whole_final = pltpu.make_async_copy(final, final_own, local_sem.at[2])
    whole_final.start()

    barrier = pltpu.get_barrier_semaphore()

    def greet_plane(k):
        pl.semaphore_signal(barrier, inc=1, device_id=(l, in_plane(k), d), device_id_type=MESH)

    def greet_column(k):
        m = in_column(k)
        pl.semaphore_signal(
            barrier, inc=1, device_id=(lax.div(m, BLOCKS), v, lax.rem(m, BLOCKS)), device_id_type=MESH
        )

    each(1, GROUPS, greet_plane)
    each(1, NCOL, greet_column)

    def product(n):
        at = aligned(n * 256, 256)
        value = jnp.dot(hidden[...], translator[:, at], preferred_element_type=f32)
        partial[:, :, :, at] = value.reshape(SIDE, SIDE, ROWS, 256)

    each(0, BLOCK // 256, product)
    pl.semaphore_wait(barrier, GROUPS - 1 + NCOL - 1)

    def rows_of(s, k):
        return aligned(s * HALF + k * CHUNK, CHUNK)

    def chain_copy(s, j, k, from_own):
        rows = rows_of(s, k)
        ll, dd = (up_l, up_d) if s == 0 else (down_l, down_d)
        if from_own:
            src = head.at[rows, cols((1 - h) * 2 + (c if j == 0 else 1 - c))]
            dst = heads.at[d, rows, :] if j == 0 else passing.at[rows, :]
        else:
            src = heads.at[opp, rows, :] if j == 0 else passing.at[rows, :]
            dst = src
        return remote(src, dst, chain_send.at[s, j, k], chain_recv.at[s, j, k], ll, v, dd)

    ends = (l == LAYERS - 1, l == 0)
    relays = (l != LAYERS - 1, l != 0)

    def source(s):
        def one(k):
            chain_copy(s, 0, k, True).start()
            chain_copy(s, 1, k, True).start()

        @pl.when(ends[s])
        def _():
            each(0, CHUNKS, one)

    def chain_sent(k):
        for s in (0, 1):
            chain_copy(s, 0, k, False).wait_send()
            chain_copy(s, 1, k, False).wait_send()
            sent(passing.at[rows_of(s, k), :], pass_send.at[s, k])

    leaving.append(lambda: each(0, CHUNKS, chain_sent))
    lag = (LAG * l, LAG * (LAYERS - 1 - l))
    TURNS = CHUNKS + LAG * (LAYERS - 1)
    done = [0]

    def chain(until):
        def one(turn):
            for s in (0, 1):
                k = turn - lag[s]

                @pl.when(jnp.logical_and(k >= 0, k < CHUNKS))
                def _(s=s, k=k):
                    rows = rows_of(s, k)
                    arrive(heads.at[opp, rows, :], chain_recv.at[s, 0, k])
                    arrive(passing.at[rows, :], chain_recv.at[s, 1, k])

                    @pl.when(relays[s])
                    def _():
                        chain_copy(s, 0, k, False).start()
                        chain_copy(s, 1, k, False).start()

                    remote(
                        passing.at[rows, :], heads.at[opp, rows, :],
                        pass_send.at[s, k], pass_recv.at[s, k], l, v, sib,
                    ).start()

        hi = int(TURNS * until)
        each(done[0], hi, one)
        done[0] = hi

    def final_copy(k):
        m = in_column(k)
        ll, dd = lax.div(m, BLOCKS), lax.rem(m, BLOCKS)
        return remote(
            final.at[:, cols(dd)], target.at[own_rows_final, :],
            fin_send.at[k], fin_recv.at[column], ll, v, dd,
        )

    left = pl.ds(0, HALF)
    right = pl.ds(HALF, HALF)

    def at_x(k):
        return y * SIDE + along_x(k)

    def at_y(k):
        return along_y(k) * SIDE + x

    def sums_start(src, part, send, recv):
        start_each(
            SIDE,
            lambda k: remote(
                src.at[:, along_x(k), :, left], part.at[0, x], send.at[0, k], recv.at[0, x], l, at_x(k), d
            ),
            send.at[0], part.at[0, 0],
        )
        start_each(
            SIDE,
            lambda k: remote(
                src.at[along_y(k), :, :, right], part.at[1, y], send.at[1, k], recv.at[1, y], l, at_y(k), d
            ),
            send.at[1], part.at[0, 0],
        )

    def sums_middle(src, part, mid, end, send, recv):
        each(1, SIDE, lambda k: arrive(part.at[0, along_x(k)], recv.at[0, along_x(k)]))
        for n in range(SIDE):
            value = src[n, x, :, left].astype(f32)
            for k in range(1, SIDE):
                value += part[0, along_x(k), n].astype(f32)
            mid[0, n] = value.astype(mid.dtype)
        start_each(
            SIDE,
            lambda k: remote(
                mid.at[0, along_y(k)], end.at[0, y], send.at[2, k], recv.at[2, y], l, at_y(k), d
            ),
            send.at[2], end.at[0, 0],
        )
        each(1, SIDE, lambda k: arrive(part.at[1, along_y(k)], recv.at[1, along_y(k)]))
        for n in range(SIDE):
            value = src[y, n, :, right].astype(f32)
            for k in range(1, SIDE):
                value += part[1, along_y(k), n].astype(f32)
            mid[1, n] = value.astype(mid.dtype)
        start_each(
            SIDE,
            lambda k: remote(
                mid.at[1, along_x(k)], end.at[1, x], send.at[3, k], recv.at[3, x], l, at_x(k), d
            ),
            send.at[3], end.at[0, 0],
        )

    def sums_end(mid, end, recv):
        each(1, SIDE, lambda k: arrive(end.at[0, along_y(k)], recv.at[2, along_y(k)]))
        each(1, SIDE, lambda k: arrive(end.at[1, along_x(k)], recv.at[3, along_x(k)]))
        value_left = mid[0, y].astype(f32)
        value_right = mid[1, x].astype(f32)
        for k in range(1, SIDE):
            value_left += end[0, along_y(k)].astype(f32)
            value_right += end[1, along_x(k)].astype(f32)
        return value_left, value_right

    def gather_start(buf, send, recv):
        my_left = buf.at[y, x, :, left]
        my_right = buf.at[y, x, :, right]
        start_each(
            SIDE, lambda k: remote(my_left, my_left, send.at[0, k], recv.at[0, x], l, at_x(k), d), send.at[0], my_left
        )
        start_each(
            SIDE, lambda k: remote(my_right, my_right, send.at[1, k], recv.at[1, y], l, at_y(k), d),
            send.at[1], my_right,
        )

    def gather_middle(buf, send, recv):
        row_left = buf.at[y, :, :, left]
        column_right = buf.at[:, x, :, right]
        each(1, SIDE, lambda k: arrive(buf.at[y, along_x(k), :, left], recv.at[0, along_x(k)]))
        start_each(
            SIDE, lambda k: remote(row_left, row_left, send.at[2, k], recv.at[2, y], l, at_y(k), d),
            send.at[2], row_left,
        )
        each(1, SIDE, lambda k: arrive(buf.at[along_y(k), x, :, right], recv.at[1, along_y(k)]))
        start_each(
            SIDE, lambda k: remote(column_right, column_right, send.at[3, k], recv.at[3, x], l, at_x(k), d),
            send.at[3], column_right,
        )

    def gather_end(buf, recv):
        each(1, SIDE, lambda k: arrive(buf.at[along_y(k), :, :, left], recv.at[2, along_y(k)]))
        each(1, SIDE, lambda k: arrive(buf.at[:, along_x(k), :, right], recv.at[3, along_x(k)]))

    source(0)
    source(1)
    sums_start(partial, parts, rs_send.at[0], rs_recv.at[0])
    start_each(NCOL, final_copy, fin_send, target.at[own_rows_final, :])
    head_copy = remote(head.at[:, cols(sib)], heads.at[d], head_send, head_recv, l, v, sib)
    head_copy.start()
    leaving.append(head_copy.wait_send)

    lane = lax.broadcasted_iota(jnp.int32, (8, TILE), 1)
    own_lanes = jnp.logical_and(lane >= l * ROWS, lane < l * ROWS + ROWS)
    pad[...] = jnp.zeros((TILE, TILE), f32)
    whole_final.wait()
    wanted = final_own[...].astype(f32)
    want_top = jnp.max(wanted, axis=1, keepdims=True)
    want_sum = jnp.sum(jnp.exp(wanted - want_top), axis=1, keepdims=True)
    column_lane = lax.broadcasted_iota(jnp.int32, (ROWS, TILE), 1)
    pad[own_rows(l), :] = jnp.where(column_lane == 0, want_top, want_sum)
    top_stats[v] = pad[...].T[0:8, :]

    def plane_copy(buf, send, recv):
        return lambda k: remote(buf.at[v], buf.at[v], send.at[k], recv.at[v], l, in_plane(k), d)

    def plane_arrive(buf, recv):
        each(1, GROUPS, lambda k: arrive(buf.at[in_plane(k)], recv.at[in_plane(k)]))

    start_each(GROUPS, plane_copy(top_stats, top_send, top_recv), top_send, top_stats.at[0])
    chain(0.2)
    sums_middle(partial, parts, part_mid, part_end, rs_send.at[0], rs_recv.at[0])
    plane_arrive(top_stats, top_recv)
    all_top = jnp.max(top_stats[:, 0:1, :], axis=0)
    all_sum = jnp.sum(top_stats[:, 1:2, :] * jnp.exp(top_stats[:, 0:1, :] - all_top[None]), axis=0)
    row_lse = all_top + jnp.log(jnp.where(own_lanes[0:1, :], all_sum, 1.0))
    want_lse[column] = jnp.broadcast_to(jnp.where(own_lanes[0:1, :], row_lse, 0.0), (8, TILE))

    def want_copy(k):
        m = in_column(k)
        return remote(
            want_lse.at[column], want_lse.at[column], wl_send.at[k], wl_recv.at[column],
            lax.div(m, BLOCKS), v, lax.rem(m, BLOCKS),
        )

    start_each(NCOL, want_copy, wl_send, want_lse.at[0])

    chain(0.26)
    value_left, value_right = sums_end(part_mid, part_end, rs_recv.at[0])
    scaled[:, left] = value_left + bias[:, left]
    scaled[:, right] = value_right + bias[:, right]
    projected = scaled[...]
    squares[d] = jnp.broadcast_to(jnp.sum(projected * projected, axis=1, keepdims=True), (ROWS, 128))

    def to_blocks(buf, send, recv):
        def copy(k):
            return remote(buf.at[d], buf.at[d], send.at[k], recv.at[d], l, v, lax.rem(d + k, BLOCKS))

        start_each(BLOCKS, copy, send, buf.at[0])

    def from_blocks(buf, recv):
        def come(k):
            dd = lax.rem(d + k, BLOCKS)
            arrive(buf.at[dd], recv.at[dd])

        each(1, BLOCKS, come)

    to_blocks(squares, sq_send, sq_recv)
    chain(0.34)
    from_blocks(squares, sq_recv)
    inverse = lax.rsqrt(jnp.sum(squares[...], axis=0)[:, :1] / D + epsilon)
    scaled[...] = projected * inverse
    normed[d, y, x] = (scaled[...] * gain[...]).astype(bf16)

    mine = normed.at[d, y, x]
    opp_copy = remote(mine, mine, opp_send, opp_recv, l, v, opp)
    opp_copy.start()
    leaving.append(opp_copy.wait_send)

    def to_sibling(block, i):
        copy = remote(normed.at[block], normed.at[block], sib_send.at[i], sib_recv.at[i], l, v, sib)
        copy.start()
        leaving.append(copy.wait_send)

    here, there = normed.at[d], normed.at[opp]
    gather_start(here, ag_send.at[0], ag_recv.at[0])
    chain(0.39)
    gather_middle(here, ag_send.at[0], ag_recv.at[0])
    arrive(normed.at[opp, y, x], opp_recv)
    gather_start(there, ag_send.at[1], ag_recv.at[1])
    chain(0.44)
    gather_middle(there, ag_send.at[1], ag_recv.at[1])
    chain(0.56)
    gather_end(here, ag_recv.at[0])
    to_sibling(d, 0)
    chain(0.66)
    gather_end(there, ag_recv.at[1])
    to_sibling(opp, 1)
    own_head.wait()
    own_final.wait()

    def multiply(block, first):
        def go(n):
            at = aligned(n * 256, 256)
            value = jnp.dot(
                normed[block].reshape(TOKENS, BLOCK), heads[block, :, at], preferred_element_type=f32
            )
            if first:
                logits[:, at] = value
            else:
                logits[:, at] += value

        each(0, QUARTER // 256, go)

    multiply(d, True)
    chain(0.74)
    arrive(normed.at[sib], sib_recv.at[0])
    arrive(heads.at[sib], head_recv)
    multiply(sib, False)
    chain(1)
    multiply(opp, False)
    arrive(normed.at[opp_sib], sib_recv.at[1])

    def passed(k):
        for s in (0, 1):
            arrive(heads.at[opp_sib, rows_of(s, k), :], pass_recv.at[s, k])

    each(0, CHUNKS, passed)
    multiply(opp_sib, False)

    for t in range(TOKENS // TILE):
        have = logits[t * TILE:(t + 1) * TILE, :]
        have_top = jnp.max(have, axis=1, keepdims=True)
        have_sum = jnp.sum(jnp.exp(have - have_top), axis=1, keepdims=True)
        tile_lane = lax.broadcasted_iota(jnp.int32, (TILE, TILE), 1)
        turned = jnp.where(tile_lane == 0, have_top, have_sum).T
        stats[v, t:t + 1, :] = turned[0:1, :]
        stats[v, 4 + t:5 + t, :] = turned[1:2, :]

    start_each(GROUPS, plane_copy(stats, st_send, st_recv), st_send, stats.at[0])

    def merge(buf):
        top = jnp.max(buf[:, 0:4, :], axis=0)
        return top, jnp.sum(buf[:, 4:8, :] * jnp.exp(buf[:, 0:4, :] - top[None]), axis=0)

    plane_arrive(stats, st_recv)
    top, total = merge(stats)
    stats2[d] = jnp.concatenate([top, total], axis=0)
    to_blocks(stats2, st2_send, st2_recv)

    def final_arrived(k):
        m = in_column(k)
        ll, dd = lax.div(m, BLOCKS), lax.rem(m, BLOCKS)
        arrive(want_lse.at[m], wl_recv.at[m])
        arrive(target.at[aligned(dd * TILE + ll * ROWS, ROWS), :], fin_recv.at[m])

    each(1, NCOL, final_arrived)
    for t in range(BLOCKS):
        lse[4 + t:5 + t, :] = (
            want_lse[t, 0:1, :] + want_lse[4 + t, 0:1, :] + want_lse[8 + t, 0:1, :] + want_lse[12 + t, 0:1, :]
        )
    from_blocks(stats2, st2_recv)
    top, total = merge(stats2)
    lse[0:4, :] = top + jnp.log(total)

    cross[...] = jnp.zeros((1, QUARTER), f32)
    for t in range(BLOCKS):
        at = pl.ds(t * TILE, TILE)
        have_lse = jnp.broadcast_to(lse[t:t + 1, :], (TILE, TILE)).T[:, 0:1]
        target_lse = jnp.broadcast_to(lse[4 + t:5 + t, :], (TILE, TILE)).T[:, 0:1]
        wanted = target[at, :].astype(f32)
        have = logits[at, :]
        want = jnp.exp(wanted - target_lse)
        grad = (jnp.exp(have - have_lse) - want).astype(bf16)
        grads[at, :] = grad
        inner[at, :] = jnp.broadcast_to(
            jnp.sum(grad.astype(f32) * have, axis=1, keepdims=True), (TILE, TILE)
        )
        cross[...] += jnp.sum(want * (wanted - have), axis=0, keepdims=True)

    def back(block, write):
        def go(n):
            at = aligned(n * 256, 256)
            write(
                at,
                lax.dot_general(
                    grads[...], heads[block, at, :], (((1,), (1,)), ((), ())),
                    preferred_element_type=f32,
                ),
            )

        each(0, BLOCK // 256, go)

    def crossing_copy(i):
        return remote(crossing.at[i], crossed.at[i], gx_send.at[i], gx_recv.at[i], l, v, sib)

    for i, block in ((0, opp_sib), (1, sib)):
        def to_crossing(at, value, i=i):
            crossing[i, :, at] = value.astype(bf16)

        back(block, to_crossing)
        crossing_copy(i).start()
        leaving.append(crossing_copy(i).wait_send)

    for i, block in ((0, opp), (1, d)):
        def to_logits(at, value):
            logits[:, at] = value

        back(block, to_logits)
        arrive(crossed.at[i], gx_recv.at[i])

        def add_rows(t, i=i):
            at = aligned(t * TILE, TILE)
            value = (logits[at, :] + crossed[i, at, :].astype(f32)).astype(bf16)
            summing[i, t] = value.reshape(SIDE, ROWS, BLOCK)

        each(0, TOKENS // TILE, add_rows)
        sums_start(summing.at[i], sum_parts.at[i], rs_send.at[1 + i], rs_recv.at[1 + i])

    for t in range(BLOCKS):
        crosses[v, t:t + 1, :] = inner[t * TILE:(t + 1) * TILE, :].T[0:1, :]
    crosses[v, 4:8, :] = jnp.broadcast_to(jnp.sum(cross[...], axis=1, keepdims=True), (4, 128))
    start_each(GROUPS, plane_copy(crosses, cr_send, cr_recv), cr_send, crosses.at[0])

    for i in (0, 1):
        sums_middle(
            summing.at[i], sum_parts.at[i], sum_mid.at[i], sum_end.at[i], rs_send.at[1 + i], rs_recv.at[1 + i]
        )
        if i == 0:
            plane_arrive(crosses, cr_recv)
            crosses2[d] = jnp.sum(crosses[...], axis=0)
            to_blocks(crosses2, cr2_send, cr2_recv)

    value_left, value_right = sums_end(sum_mid.at[0], sum_end.at[0], rs_recv.at[1])
    half_sum[:, left] = value_left.astype(bf16)
    half_sum[:, right] = value_right.astype(bf16)
    go_copy = remote(half_sum, other_sum, go_send, go_recv, l, v, opp)
    go_copy.start()
    leaving.append(go_copy.wait_send)
    value_left, value_right = sums_end(sum_mid.at[1], sum_end.at[1], rs_recv.at[2])
    finals[:, left] = value_left
    finals[:, right] = value_right
    from_blocks(crosses2, cr2_recv)
    crossed_all = jnp.sum(crosses2[...], axis=0)
    div_out[0] = (jnp.sum(crossed_all[4:5, 0:1]) + jnp.sum(lse[0:4, :] - lse[4:8, :])) / TOKENS
    lse[...] = crossed_all
    pad[...] = jnp.broadcast_to(lse[pl.ds(y, 1), :], (TILE, TILE)).T
    inner_mean = pad[own_rows(x), :][:, 0:1] / D
    arrive(other_sum, go_recv)

    grad_scaled = (finals[...] + other_sum[...].astype(f32)) * gain[...]
    inverse = lax.rsqrt(jnp.sum(squares[...], axis=0)[:, :1] / D + epsilon)
    gathered_grad[y, x] = (inverse * (grad_scaled - scaled[...] * inner_mean)).astype(bf16)
    gather_start(gathered_grad, ag_send.at[2], ag_recv.at[2])
    gather_middle(gathered_grad, ag_send.at[2], ag_recv.at[2])
    gather_end(gathered_grad, ag_recv.at[2])

    def outputs(n):
        at = aligned(n * 256, 256)
        grad = gathered_grad[:, :, :, at].reshape(TOKENS, 256)
        weights_out[0, :, at] = lax.dot_general(
            hidden[...], grad, (((0,), (0,)), ((), ())), preferred_element_type=f32
        )
        offsets_out[:, at] = jnp.sum(grad.astype(f32), axis=0, keepdims=True)

    each(0, BLOCK // 256, outputs)
    drain()


def run(hidden, translator, bias, gain, head, final):
    dma = pltpu.SemaphoreType.DMA
    vmem = pltpu.VMEM
    in_vmem = pl.BlockSpec(memory_space=pltpu.VMEM)
    anywhere = pl.BlockSpec(memory_space=pl.ANY)
    width = hidden.shape[1]
    return pl.pallas_call(
        kernel,
        out_shape=[
            jax.ShapeDtypeStruct((1, width, BLOCK), f32),
            jax.ShapeDtypeStruct((1, BLOCK), f32),
            jax.ShapeDtypeStruct((1,), f32),
        ],
        in_specs=[in_vmem] * 4 + [anywhere] * 2,
        out_specs=[in_vmem] * 2 + [pl.BlockSpec(memory_space=pltpu.SMEM)],
        scratch_shapes=[
            vmem((BLOCKS, BLOCK, QUARTER), bf16),
            vmem((BLOCK, QUARTER), bf16),
            vmem((BLOCKS, SIDE, SIDE, ROWS, BLOCK), bf16),
            vmem((SIDE, SIDE, ROWS, BLOCK), f32),
            vmem((TOKENS, QUARTER), bf16),
            vmem((ROWS, BLOCKS * QUARTER), bf16),
            vmem((TILE, TILE), f32),
            vmem((ROWS, BLOCK), f32),
            vmem((BLOCKS, ROWS, 128), f32),
            vmem((TOKENS, QUARTER), f32),
            vmem((GROUPS, 8, TILE), f32),
            vmem((LAYERS * BLOCKS, 8, TILE), f32),
            vmem((GROUPS, 8, TILE), f32),
            vmem((BLOCKS, 8, TILE), f32),
            vmem((8, TILE), f32),
            vmem((1, QUARTER), f32),
            vmem((TOKENS, TILE), f32),
            vmem((GROUPS, 8, TILE), f32),
            vmem((BLOCKS, 8, TILE), f32),
            vmem((TOKENS, QUARTER), bf16),
            vmem((2, TOKENS, BLOCK), bf16),
            vmem((2, TOKENS, BLOCK), bf16),
            vmem((2, SIDE, SIDE, ROWS, BLOCK), bf16),
            vmem((2, SIDE, SIDE, ROWS, HALF), f32),
            vmem((2, SIDE, ROWS, HALF), f32),
            vmem((2, SIDE, ROWS, HALF), f32),
            vmem((2, 2, SIDE, SIDE, ROWS, HALF), bf16),
            vmem((2, 2, SIDE, ROWS, HALF), bf16),
            vmem((2, 2, SIDE, ROWS, HALF), bf16),
            vmem((ROWS, BLOCK), bf16),
            vmem((ROWS, BLOCK), bf16),
            vmem((ROWS, BLOCK), f32),
            vmem((SIDE, SIDE, ROWS, BLOCK), bf16),
            dma((2, 2, CHUNKS)), dma((2, 2, CHUNKS)),
            dma((2, CHUNKS)), dma((2, CHUNKS)),
            dma, dma,
            dma((16,)), dma((16,)),
            dma((BLOCKS,)), dma((BLOCKS,)),
            dma, dma,
            dma((2,)), dma((2,)),
            dma((GROUPS,)), dma((GROUPS,)),
            dma((16,)), dma((16,)),
            dma((GROUPS,)), dma((GROUPS,)),
            dma((BLOCKS,)), dma((BLOCKS,)),
            dma((GROUPS,)), dma((GROUPS,)),
            dma((BLOCKS,)), dma((BLOCKS,)),
            dma((2,)), dma((2,)),
            dma((3, 4, SIDE)), dma((3, 4, SIDE)),
            dma((3, 4, SIDE)), dma((3, 4, SIDE)),
            dma, dma,
            dma((3,)),
        ],
        compiler_params=pltpu.CompilerParams(
            collective_id=0, has_side_effects=True, vmem_limit_bytes=56 * 1024 * 1024
        ),
        name="lens",
    )(hidden, translator, bias, gain, head, final)


def shards(hidden, translator, bias, gain, head, final_logits):
    return tuple(run(hidden[0], translator[0], bias, gain[None], head, final_logits[0]))


def solution(mesh):
    in_specs = (
        P("layer", None, "vocab"),
        P("layer", "vocab", "dp"),
        P("layer", "dp"),
        P("dp"),
        P("dp", "vocab"),
        P("dp", "layer", "vocab"),
    )
    out_specs = (P("layer", "vocab", "dp"), P("layer", "dp"), P("layer"))
    return jax.shard_map(shards, mesh=mesh, in_specs=in_specs, out_specs=out_specs, check_vma=False)
```

time: 195 us -> 168 us (0.86)
  Pallas kernels: 188 us -> 161 us
  other arithmetic: 2 us -> 0 us
    pallas_call x1, Pallas kernels: 188 us -> 161 us  [run(): pl.pallas_call(kernel, out_shape=[jax.ShapeDtypeStruct((1, width, BLOCK),...]
    unnamed x3 -> x2, local copies, waits for them, and re-layouts: 1.31 us -> 3.58 us
    reduce_sum x1 -> x0, other arithmetic: 2 us -> none  [shards(): grad_offsets = jnp.sum(grad_projected.astype(f32), axis=0)]
where the time goes in v3:
time: 168 us; the launch traced here: 167 us
  Pallas kernels  161 us (96%)
  local copies, waits for them, and re-layouts  3.58 us (2%)
  between operations  2.4 us (1%)
    pallas_call x1, Pallas kernels, run(): pl.pallas_call(kernel, out_shape=[jax.ShapeDtypeStruct((1, width, BLOCK),...  161 us
    unnamed x2, local copies, waits for them, and re-layouts  3.58 us

profile of v3, /device:TPU:1, one launch (start us, length us, event | category | flops | bytes accessed | tf_op | source)
XLA Modules:
  0.0 167.4 jit_solution(16919946207326003408)
XLA Ops:
  0.6 161.5 %lens.1 = (f32[1,256,1024]{2,1,0:T(8,128)}, f32[1,1024]{1,0:T(1,128)}, f32[1]{0:T(128)}) custom-call(bf16[512,256]{1,0:T(8,128)(2,1)} %bitcast.5, bf16[256,1024]{1,0:T(8,128)(2,1)} %bitcast.4, f32[1,1024]{1,0:T(1,128)} %bias.1, f32[1,1024]{1,0:T(1,128)} %bitcast.7, bf16[1024,4096]{1,0:T(8,128)(2,1)} %head.1, bf16[32,4096]{1,0:T(8,128)(2,1)} %bitcast.6), custom_call_target="tpu_custom_call" | custom-call | tf_op jit(solution)/shard_map/lens/pallas_call | solution.py:572
  162.1 2.3 %copy.12 = f32[1,256,1024]{2,1,0:T(8,128)} copy(f32[1,256,1024]{2,1,0:T(8,128)} %get-tuple-element.6) | data formatting | bytes 2097152
  164.4 1.3 copy.13

commit v4 on v3

--- a/solution.py
+++ b/solution.py
@@ -19,6 +19,8 @@
 CHUNK = 16
 CHUNKS = HALF // CHUNK
 LAG = 3
+FINALS = 2 * ROWS // CHUNK
+PACE = (0.22, 0.3, 0.4, 0.48, 0.55, 0.75, 0.85, 0.9)
 
 epsilon = 1e-05
 f32 = jnp.float32
@@ -39,11 +41,13 @@
 
 
 def kernel(
-    hidden, translator, bias, gain, head, final, weights_out, offsets_out, div_out,
+    hidden, translator, bias, gain, head, final, gathered_grad, div_out,
     heads, passing, normed, partial, target, final_own, pad, scaled, squares, logits,
     top_stats, want_lse, stats, stats2, lse, cross, inner, crosses, crosses2, grads, crossing, crossed, summing,
-    parts, part_mid, part_end, sum_parts, sum_mid, sum_end, half_sum, other_sum, finals, gathered_grad,
-    chain_send, chain_recv, pass_send, pass_recv, head_send, head_recv, fin_send, fin_recv,
+    parts, part_mid, part_end, sum_parts, sum_mid, sum_end, half_sum, other_sum, finals,
+    next_final, passing_final,
+    chain_send, chain_recv, pass_send, pass_recv, fchain_send, fchain_recv, fpass_send, fpass_recv,
+    next_send, next_recv, head_send, head_recv, fin_send, fin_recv,
     sq_send, sq_recv, opp_send, opp_recv, sib_send, sib_recv,
     top_send, top_recv, wl_send, wl_recv, st_send, st_recv, st2_send, st2_recv, cr_send, cr_recv,
     cr2_send, cr2_recv, gx_send, gx_recv, rs_send, rs_recv, ag_send, ag_recv,
@@ -162,13 +166,58 @@
         def _():
             each(0, CHUNKS, one)
 
+    def final_at(s, k):
+        return (LAYERS - 1 - lax.div(k, 2) if s == 0 else lax.div(k, 2)) * ROWS + lax.rem(k, 2) * CHUNK
+
+    def final_rows(s, k, block):
+        return aligned(block * TILE + final_at(s, k), CHUNK)
+
+    def final_chain(s, j, k, src, block):
+        ll, dd = (up_l, up_d) if s == 0 else (down_l, down_d)
+        dst = target.at[final_rows(s, k, block), :] if j == 0 else passing_final.at[aligned(final_at(s, k), CHUNK), :]
+        return remote(
+            dst if src is None else src, dst, fchain_send.at[s, j, k], fchain_recv.at[s, j, k], ll, v, dd
+        )
+
+    def final_source(s, lo, hi):
+        def one(k):
+            rows = aligned(lax.rem(k, 2) * CHUNK, CHUNK)
+            for j in (0, 1):
+                q = c if j == 0 else 1 - c
+                if lo == 0:
+                    src = final.at[rows, cols((1 - h) * 2 + q)]
+                else:
+                    src = next_final.at[rows, cols(q)]
+                final_chain(s, j, k, src, d).start()
+
+        each(lo, hi, one)
+
+    next_copy = remote(
+        final.at[:, aligned((1 - h) * 2 * QUARTER, 2 * QUARTER)], next_final, next_send, next_recv, 3 * (l - 1), v, d
+    )
+    inner_layer = jnp.logical_and(l > 0, l < LAYERS - 1)
+
+    def next_sent():
+        @pl.when(inner_layer)
+        def _():
+            next_copy.wait_send()
+
+    leaving.append(next_sent)
+
     def chain_sent(k):
         for s in (0, 1):
             chain_copy(s, 0, k, False).wait_send()
             chain_copy(s, 1, k, False).wait_send()
             sent(passing.at[rows_of(s, k), :], pass_send.at[s, k])
 
+    def final_chain_sent(k):
+        for s in (0, 1):
+            final_chain(s, 0, k, None, opp).wait_send()
+            final_chain(s, 1, k, None, opp).wait_send()
+            sent(passing_final.at[0:CHUNK, :], fpass_send.at[s, k])
+
     leaving.append(lambda: each(0, CHUNKS, chain_sent))
+    leaving.append(lambda: each(0, FINALS, final_chain_sent))
     lag = (LAG * l, LAG * (LAYERS - 1 - l))
     TURNS = CHUNKS + LAG * (LAYERS - 1)
     done = [0]
@@ -194,16 +243,35 @@
                         pass_send.at[s, k], pass_recv.at[s, k], l, v, sib,
                     ).start()
 
-        hi = int(TURNS * until)
+                @pl.when(jnp.logical_and(k >= CHUNKS, k < CHUNKS + FINALS))
+                def _(s=s, k=k - CHUNKS):
+                    rows = final_rows(s, k, opp)
+                    passed_rows = passing_final.at[aligned(final_at(s, k), CHUNK), :]
+                    arrive(target.at[rows, :], fchain_recv.at[s, 0, k])
+                    arrive(passed_rows, fchain_recv.at[s, 1, k])
+
+                    @pl.when(relays[s])
+                    def _():
+                        final_chain(s, 0, k, None, opp).start()
+                        final_chain(s, 1, k, None, opp).start()
+
+                    remote(
+                        passed_rows, target.at[rows, :], fpass_send.at[s, k], fpass_recv.at[s, k], l, v, sib
+                    ).start()
+
+        hi = min(int(TURNS * until), TURNS + FINALS)
         each(done[0], hi, one)
         done[0] = hi
 
+    HALF_COLUMN = LAYERS * 2
+    in_half = l * 2 + c
+
     def final_copy(k):
-        m = in_column(k)
-        ll, dd = lax.div(m, BLOCKS), lax.rem(m, BLOCKS)
+        m = lax.rem(in_half + k, HALF_COLUMN)
+        dd = h * 2 + lax.rem(m, 2)
         return remote(
             final.at[:, cols(dd)], target.at[own_rows_final, :],
-            fin_send.at[k], fin_recv.at[column], ll, v, dd,
+            fin_send.at[k], fin_recv.at[in_half], lax.div(m, 2), v, dd,
         )
 
     left = pl.ds(0, HALF)
@@ -298,10 +366,18 @@
         each(1, SIDE, lambda k: arrive(buf.at[along_y(k), :, :, left], recv.at[2, along_y(k)]))
         each(1, SIDE, lambda k: arrive(buf.at[:, along_x(k), :, right], recv.at[3, along_x(k)]))
 
+    @pl.when(inner_layer)
+    def _():
+        next_copy.start()
+
     source(0)
     source(1)
+    for s in (0, 1):
+        @pl.when(ends[s])
+        def _(s=s):
+            final_source(s, 0, 2)
+
     sums_start(partial, parts, rs_send.at[0], rs_recv.at[0])
-    start_each(NCOL, final_copy, fin_send, target.at[own_rows_final, :])
     head_copy = remote(head.at[:, cols(sib)], heads.at[d], head_send, head_recv, l, v, sib)
     head_copy.start()
     leaving.append(head_copy.wait_send)
@@ -324,7 +400,13 @@
         each(1, GROUPS, lambda k: arrive(buf.at[in_plane(k)], recv.at[in_plane(k)]))
 
     start_each(GROUPS, plane_copy(top_stats, top_send, top_recv), top_send, top_stats.at[0])
-    chain(0.2)
+    chain(PACE[0])
+    for s in (0, 1):
+        @pl.when(ends[s])
+        def _(s=s):
+            arrive(next_final, next_recv)
+            final_source(s, 2, FINALS)
+
     sums_middle(partial, parts, part_mid, part_end, rs_send.at[0], rs_recv.at[0])
     plane_arrive(top_stats, top_recv)
     all_top = jnp.max(top_stats[:, 0:1, :], axis=0)
@@ -341,7 +423,7 @@
 
     start_each(NCOL, want_copy, wl_send, want_lse.at[0])
 
-    chain(0.26)
+    chain(PACE[1])
     value_left, value_right = sums_end(part_mid, part_end, rs_recv.at[0])
     scaled[:, left] = value_left + bias[:, left]
     scaled[:, right] = value_right + bias[:, right]
@@ -362,7 +444,7 @@
         each(1, BLOCKS, come)
 
     to_blocks(squares, sq_send, sq_recv)
-    chain(0.34)
+    chain(PACE[2])
     from_blocks(squares, sq_recv)
     inverse = lax.rsqrt(jnp.sum(squares[...], axis=0)[:, :1] / D + epsilon)
     scaled[...] = projected * inverse
@@ -380,16 +462,16 @@
 
     here, there = normed.at[d], normed.at[opp]
     gather_start(here, ag_send.at[0], ag_recv.at[0])
-    chain(0.39)
+    chain(PACE[3])
     gather_middle(here, ag_send.at[0], ag_recv.at[0])
     arrive(normed.at[opp, y, x], opp_recv)
     gather_start(there, ag_send.at[1], ag_recv.at[1])
-    chain(0.44)
+    chain(PACE[4])
     gather_middle(there, ag_send.at[1], ag_recv.at[1])
-    chain(0.56)
+    chain(PACE[5])
     gather_end(here, ag_recv.at[0])
     to_sibling(d, 0)
-    chain(0.66)
+    chain(PACE[6])
     gather_end(there, ag_recv.at[1])
     to_sibling(opp, 1)
     own_head.wait()
@@ -409,11 +491,12 @@
         each(0, QUARTER // 256, go)
 
     multiply(d, True)
-    chain(0.74)
+    chain(PACE[7])
     arrive(normed.at[sib], sib_recv.at[0])
     arrive(heads.at[sib], head_recv)
     multiply(sib, False)
     chain(1)
+    start_each(HALF_COLUMN, final_copy, fin_send, target.at[own_rows_final, :])
     multiply(opp, False)
     arrive(normed.at[opp_sib], sib_recv.at[1])
 
@@ -439,18 +522,28 @@
         top = jnp.max(buf[:, 0:4, :], axis=0)
         return top, jnp.sum(buf[:, 4:8, :] * jnp.exp(buf[:, 0:4, :] - top[None]), axis=0)
 
+    chain(2)
     plane_arrive(stats, st_recv)
     top, total = merge(stats)
     stats2[d] = jnp.concatenate([top, total], axis=0)
     to_blocks(stats2, st2_send, st2_recv)
 
+    def want_arrived(k):
+        m = in_column(k)
+        arrive(want_lse.at[m], wl_recv.at[m])
+
     def final_arrived(k):
-        m = in_column(k)
-        ll, dd = lax.div(m, BLOCKS), lax.rem(m, BLOCKS)
-        arrive(want_lse.at[m], wl_recv.at[m])
-        arrive(target.at[aligned(dd * TILE + ll * ROWS, ROWS), :], fin_recv.at[m])
-
-    each(1, NCOL, final_arrived)
+        m = lax.rem(in_half + k, HALF_COLUMN)
+        rows = aligned((h * 2 + lax.rem(m, 2)) * TILE + lax.div(m, 2) * ROWS, ROWS)
+        arrive(target.at[rows, :], fin_recv.at[m])
+
+    def final_passed(k):
+        for s in (0, 1):
+            arrive(target.at[final_rows(s, k, opp_sib), :], fpass_recv.at[s, k])
+
+    each(1, NCOL, want_arrived)
+    each(1, HALF_COLUMN, final_arrived)
+    each(0, FINALS, final_passed)
     for t in range(BLOCKS):
         lse[4 + t:5 + t, :] = (
             want_lse[t, 0:1, :] + want_lse[4 + t, 0:1, :] + want_lse[8 + t, 0:1, :] + want_lse[12 + t, 0:1, :]
@@ -551,16 +644,16 @@
     gather_middle(gathered_grad, ag_send.at[2], ag_recv.at[2])
     gather_end(gathered_grad, ag_recv.at[2])
 
-    def outputs(n):
-        at = aligned(n * 256, 256)
-        grad = gathered_grad[:, :, :, at].reshape(TOKENS, 256)
-        weights_out[0, :, at] = lax.dot_general(
-            hidden[...], grad, (((0,), (0,)), ((), ())), preferred_element_type=f32
-        )
-        offsets_out[:, at] = jnp.sum(grad.astype(f32), axis=0, keepdims=True)
-
-    each(0, BLOCK // 256, outputs)
     drain()
+
+
+def products(hidden, grad, divergence, weights_out, offsets_out, div_out):
+    value = grad[...].reshape(TOKENS, grad.shape[-1])
+    weights_out[0] = lax.dot_general(
+        hidden[...], value, (((0,), (0,)), ((), ())), preferred_element_type=f32
+    )
+    offsets_out[...] = jnp.sum(value.astype(f32), axis=0, keepdims=True)
+    div_out[0] = divergence[0]
 
 
 def run(hidden, translator, bias, gain, head, final):
@@ -569,15 +662,15 @@
     in_vmem = pl.BlockSpec(memory_space=pltpu.VMEM)
     anywhere = pl.BlockSpec(memory_space=pl.ANY)
     width = hidden.shape[1]
-    return pl.pallas_call(
+    smem = pl.BlockSpec(memory_space=pltpu.SMEM)
+    grad, divergence = pl.pallas_call(
         kernel,
         out_shape=[
-            jax.ShapeDtypeStruct((1, width, BLOCK), f32),
-            jax.ShapeDtypeStruct((1, BLOCK), f32),
+            jax.ShapeDtypeStruct((SIDE, SIDE, ROWS, BLOCK), bf16),
             jax.ShapeDtypeStruct((1,), f32),
         ],
         in_specs=[in_vmem] * 4 + [anywhere] * 2,
-        out_specs=[in_vmem] * 2 + [pl.BlockSpec(memory_space=pltpu.SMEM)],
+        out_specs=[in_vmem, smem],
         scratch_shapes=[
             vmem((BLOCKS, BLOCK, QUARTER), bf16),
             vmem((BLOCK, QUARTER), bf16),
@@ -611,9 +704,13 @@
             vmem((ROWS, BLOCK), bf16),
             vmem((ROWS, BLOCK), bf16),
             vmem((ROWS, BLOCK), f32),
-            vmem((SIDE, SIDE, ROWS, BLOCK), bf16),
+            vmem((ROWS, 2 * QUARTER), bf16),
+            vmem((TILE, QUARTER), bf16),
             dma((2, 2, CHUNKS)), dma((2, 2, CHUNKS)),
             dma((2, CHUNKS)), dma((2, CHUNKS)),
+            dma((2, 2, FINALS)), dma((2, 2, FINALS)),
+            dma((2, FINALS)), dma((2, FINALS)),
+            dma, dma,
             dma, dma,
             dma((16,)), dma((16,)),
             dma((BLOCKS,)), dma((BLOCKS,)),
@@ -636,6 +733,27 @@
         ),
         name="lens",
     )(hidden, translator, bias, gain, head, final)
+    tile = 256
+    return pl.pallas_call(
+        products,
+        out_shape=[
+            jax.ShapeDtypeStruct((1, width, BLOCK), f32),
+            jax.ShapeDtypeStruct((1, BLOCK), f32),
+            jax.ShapeDtypeStruct((1,), f32),
+        ],
+        grid=(BLOCK // tile,),
+        in_specs=[
+            pl.BlockSpec((TOKENS, width), lambda n: (0, 0)),
+            pl.BlockSpec((SIDE, SIDE, ROWS, tile), lambda n: (0, 0, 0, n)),
+            smem,
+        ],
+        out_specs=[
+            pl.BlockSpec((1, width, tile), lambda n: (0, 0, n)),
+            pl.BlockSpec((1, tile), lambda n: (0, n)),
+            smem,
+        ],
+        name="products",
+    )(hidden, grad, divergence)
 
 
 def shards(hidden, translator, bias, gain, head, final_logits):

time: 168 us -> 153 us (0.911); the launches traced: 167 us -> 150 us
  Pallas kernels: 161 us -> 149 us
  local copies, waits for them, and re-layouts: 3.58 us -> 0 us
  between operations: 2.4 us -> 0.64 us
    pallas_call x1 -> x2, Pallas kernels: 161 us -> 149 us  [the longest x1 145 us: run(): pl.pallas_call(kernel, out_shape=[jax.ShapeDtypeStruct((SIDE, SIDE, ROWS,...]
    unnamed x2 -> x0, local copies, waits for them, and re-layouts: 3.58 us -> none
where the time goes in v4:
time: 153 us; the launch traced here: 150 us
  Pallas kernels  149 us (97%)
    pallas_call x1, Pallas kernels, run(): pl.pallas_call(kernel, out_shape=[jax.ShapeDtypeStruct((SIDE, SIDE, ROWS,...  145 us
    pallas_call x1, Pallas kernels, run(): pl.pallas_call(products, out_shape=[jax.ShapeDtypeStruct((1, width, BLOCK...  4.53 us

profile of v4, /device:TPU:1, one launch (start us, length us, event | category | flops | bytes accessed | tf_op | source)
XLA Modules:
  0.0 149.9 jit_solution(11556264585825180549)
XLA Ops:
  0.6 144.7 %lens.1 = (bf16[4,4,32,1024]{3,2,1,0:T(8,128)(2,1)}, f32[1]{0:T(128)}) custom-call(bf16[512,256]{1,0:T(8,128)(2,1)} %bitcast.4, bf16[256,1024]{1,0:T(8,128)(2,1)} %bitcast.6, f32[1,1024]{1,0:T(1,128)} %bias.1, f32[1,1024]{1,0:T(1,128)} %bitcast.8, bf16[1024,4096]{1,0:T(8,128)(2,1)} %head.1, bf16[32,4096]{1,0:T(8,128)(2,1)} %bitcast.7), custom_call_target="tpu_custom_call" | custom-call | tf_op jit(solution)/shard_map/lens/pallas_call | solution.py:666
  145.4 4.5 %products.1 = (f32[1,256,1024]{2,1,0:T(8,128)}, f32[1,1024]{1,0:T(1,128)}, f32[1]{0:T(128)}) custom-call(bf16[512,256]{1,0:T(8,128)(2,1)} %bitcast.5, bf16[4,4,32,1024]{3,2,1,0:T(8,128)(2,1)} %get-tuple-element.5.grad, f32[1]{0:T(128)} %get-tuple-element.6.divergence), custom_call_target="tpu_custom_call" | custom-call | tf_op jit(solution)/shard_map/products/pallas_call | solution.py:737

commit v5 on v4

--- a/solution.py
+++ b/solution.py
@@ -16,11 +16,11 @@
 ROWS = TOKENS // GROUPS
 TILE = 128
 HALF = BLOCK // 2
-CHUNK = 16
+CHUNK = 32
 CHUNKS = HALF // CHUNK
 LAG = 3
 FINALS = 2 * ROWS // CHUNK
-PACE = (0.22, 0.3, 0.4, 0.48, 0.55, 0.75, 0.85, 0.9)
+PACE = (0.3, 0.4, 0.5, 0.58, 0.64, 0.82, 0.9, 0.92, 0.94, 0.96, 0.98, 1.0)
 
 epsilon = 1e-05
 f32 = jnp.float32
@@ -41,8 +41,9 @@
 
 
 def kernel(
-    hidden, translator, bias, gain, head, final, gathered_grad, div_out,
-    heads, passing, normed, partial, target, final_own, pad, scaled, squares, logits,
+    hidden_hbm, translator_hbm, bias_hbm, gain_hbm, head, final, gathered_grad, turned, div_out,
+    hidden, translator, bias, gain,
+    heads, normed, partial, target, final_own, pad, scaled, squares, logits,
     top_stats, want_lse, stats, stats2, lse, cross, inner, crosses, crosses2, grads, crossing, crossed, summing,
     parts, part_mid, part_end, sum_parts, sum_mid, sum_end, half_sum, other_sum, finals,
     next_final, passing_final,
@@ -110,6 +111,14 @@
     def own_rows(p):
         return aligned(p * ROWS, ROWS)
 
+    staged = [
+        pltpu.make_async_copy(src, dst, local_sem.at[3 + n])
+        for n, (src, dst) in enumerate(
+            ((hidden_hbm, hidden), (translator_hbm, translator), (bias_hbm, bias), (gain_hbm, gain))
+        )
+    ]
+    for copy in staged:
+        copy.start()
     own_head = pltpu.make_async_copy(head.at[:, cols(d)], heads.at[d], local_sem.at[0])
     own_head.start()
     own_rows_final = aligned(d * TILE + l * ROWS, ROWS)
@@ -137,20 +146,25 @@
         value = jnp.dot(hidden[...], translator[:, at], preferred_element_type=f32)
         partial[:, :, :, at] = value.reshape(SIDE, SIDE, ROWS, 256)
 
+    for copy in staged:
+        copy.wait()
     each(0, BLOCK // 256, product)
     pl.semaphore_wait(barrier, GROUPS - 1 + NCOL - 1)
 
     def rows_of(s, k):
         return aligned(s * HALF + k * CHUNK, CHUNK)
+
+    def slot(j):
+        return opp + j * (BLOCKS - opp)
 
     def chain_copy(s, j, k, from_own):
         rows = rows_of(s, k)
         ll, dd = (up_l, up_d) if s == 0 else (down_l, down_d)
         if from_own:
             src = head.at[rows, cols((1 - h) * 2 + (c if j == 0 else 1 - c))]
-            dst = heads.at[d, rows, :] if j == 0 else passing.at[rows, :]
+            dst = heads.at[d if j == 0 else BLOCKS, rows, :]
         else:
-            src = heads.at[opp, rows, :] if j == 0 else passing.at[rows, :]
+            src = heads.at[slot(j), rows, :]
             dst = src
         return remote(src, dst, chain_send.at[s, j, k], chain_recv.at[s, j, k], ll, v, dd)
 
@@ -167,7 +181,7 @@
             each(0, CHUNKS, one)
 
     def final_at(s, k):
-        return (LAYERS - 1 - lax.div(k, 2) if s == 0 else lax.div(k, 2)) * ROWS + lax.rem(k, 2) * CHUNK
+        return (LAYERS - 1 - k if s == 0 else k) * ROWS
 
     def final_rows(s, k, block):
         return aligned(block * TILE + final_at(s, k), CHUNK)
@@ -181,7 +195,7 @@
 
     def final_source(s, lo, hi):
         def one(k):
-            rows = aligned(lax.rem(k, 2) * CHUNK, CHUNK)
+            rows = aligned(0, CHUNK)
             for j in (0, 1):
                 q = c if j == 0 else 1 - c
                 if lo == 0:
@@ -208,7 +222,7 @@
         for s in (0, 1):
             chain_copy(s, 0, k, False).wait_send()
             chain_copy(s, 1, k, False).wait_send()
-            sent(passing.at[rows_of(s, k), :], pass_send.at[s, k])
+            sent(heads.at[BLOCKS, rows_of(s, k), :], pass_send.at[s, k])
 
     def final_chain_sent(k):
         for s in (0, 1):
@@ -219,47 +233,58 @@
     leaving.append(lambda: each(0, CHUNKS, chain_sent))
     leaving.append(lambda: each(0, FINALS, final_chain_sent))
     lag = (LAG * l, LAG * (LAYERS - 1 - l))
-    TURNS = CHUNKS + LAG * (LAYERS - 1)
+    TURNS = 2 * CHUNKS + LAG * (LAYERS - 1)
     done = [0]
 
     def chain(until):
         def one(turn):
             for s in (0, 1):
-                k = turn - lag[s]
-
-                @pl.when(jnp.logical_and(k >= 0, k < CHUNKS))
-                def _(s=s, k=k):
+                u = turn - lag[s]
+
+                @pl.when(jnp.logical_and(u >= 0, u < 2 * CHUNKS))
+                def _(s=s, u=u):
+                    k, j = lax.div(u, 2), lax.rem(u, 2)
                     rows = rows_of(s, k)
-                    arrive(heads.at[opp, rows, :], chain_recv.at[s, 0, k])
-                    arrive(passing.at[rows, :], chain_recv.at[s, 1, k])
+                    arrive(heads.at[slot(j), rows, :], chain_recv.at[s, j, k])
 
                     @pl.when(relays[s])
                     def _():
-                        chain_copy(s, 0, k, False).start()
-                        chain_copy(s, 1, k, False).start()
-
-                    remote(
-                        passing.at[rows, :], heads.at[opp, rows, :],
-                        pass_send.at[s, k], pass_recv.at[s, k], l, v, sib,
-                    ).start()
-
-                @pl.when(jnp.logical_and(k >= CHUNKS, k < CHUNKS + FINALS))
-                def _(s=s, k=k - CHUNKS):
+                        chain_copy(s, j, k, False).start()
+
+                    @pl.when(j == 1)
+                    def _():
+                        remote(
+                            heads.at[BLOCKS, rows, :], heads.at[opp, rows, :],
+                            pass_send.at[s, k], pass_recv.at[s, k], l, v, sib,
+                        ).start()
+
+                @pl.when(jnp.logical_and(u >= 2 * CHUNKS, u < 2 * (CHUNKS + FINALS)))
+                def _(s=s, u=u - 2 * CHUNKS):
+                    k, j = lax.div(u, 2), lax.rem(u, 2)
                     rows = final_rows(s, k, opp)
                     passed_rows = passing_final.at[aligned(final_at(s, k), CHUNK), :]
-                    arrive(target.at[rows, :], fchain_recv.at[s, 0, k])
-                    arrive(passed_rows, fchain_recv.at[s, 1, k])
-
-                    @pl.when(relays[s])
+
+                    @pl.when(j == 0)
                     def _():
-                        final_chain(s, 0, k, None, opp).start()
-                        final_chain(s, 1, k, None, opp).start()
-
-                    remote(
-                        passed_rows, target.at[rows, :], fpass_send.at[s, k], fpass_recv.at[s, k], l, v, sib
-                    ).start()
-
-        hi = min(int(TURNS * until), TURNS + FINALS)
+                        arrive(target.at[rows, :], fchain_recv.at[s, 0, k])
+
+                        @pl.when(relays[s])
+                        def _():
+                            final_chain(s, 0, k, None, opp).start()
+
+                    @pl.when(j == 1)
+                    def _():
+                        arrive(passed_rows, fchain_recv.at[s, 1, k])
+
+                        @pl.when(relays[s])
+                        def _():
+                            final_chain(s, 1, k, None, opp).start()
+
+                        remote(
+                            passed_rows, target.at[rows, :], fpass_send.at[s, k], fpass_recv.at[s, k], l, v, sib
+                        ).start()
+
+        hi = min(int(TURNS * until), TURNS + 2 * FINALS)
         each(done[0], hi, one)
         done[0] = hi
 
@@ -283,21 +308,23 @@
     def at_y(k):
         return along_y(k) * SIDE + x
 
-    def sums_start(src, part, send, recv):
-        start_each(
-            SIDE,
-            lambda k: remote(
-                src.at[:, along_x(k), :, left], part.at[0, x], send.at[0, k], recv.at[0, x], l, at_x(k), d
-            ),
-            send.at[0], part.at[0, 0],
-        )
-        start_each(
-            SIDE,
-            lambda k: remote(
-                src.at[along_y(k), :, :, right], part.at[1, y], send.at[1, k], recv.at[1, y], l, at_y(k), d
-            ),
-            send.at[1], part.at[0, 0],
-        )
+    def sums_start(src, part, send, recv, ways=(0, 1)):
+        if 0 in ways:
+            start_each(
+                SIDE,
+                lambda k: remote(
+                    src.at[:, along_x(k), :, left], part.at[0, x], send.at[0, k], recv.at[0, x], l, at_x(k), d
+                ),
+                send.at[0], part.at[0, 0],
+            )
+        if 1 in ways:
+            start_each(
+                SIDE,
+                lambda k: remote(
+                    src.at[along_y(k), :, :, right], part.at[1, y], send.at[1, k], recv.at[1, y], l, at_y(k), d
+                ),
+                send.at[1], part.at[0, 0],
+            )
 
     def sums_middle(src, part, mid, end, send, recv):
         each(1, SIDE, lambda k: arrive(part.at[0, along_x(k)], recv.at[0, along_x(k)]))
@@ -375,7 +402,7 @@
     for s in (0, 1):
         @pl.when(ends[s])
         def _(s=s):
-            final_source(s, 0, 2)
+            final_source(s, 0, 1)
 
     sums_start(partial, parts, rs_send.at[0], rs_recv.at[0])
     head_copy = remote(head.at[:, cols(sib)], heads.at[d], head_send, head_recv, l, v, sib)
@@ -386,6 +413,7 @@
     own_lanes = jnp.logical_and(lane >= l * ROWS, lane < l * ROWS + ROWS)
     pad[...] = jnp.zeros((TILE, TILE), f32)
     whole_final.wait()
+    chain(0.1)
     wanted = final_own[...].astype(f32)
     want_top = jnp.max(wanted, axis=1, keepdims=True)
     want_sum = jnp.sum(jnp.exp(wanted - want_top), axis=1, keepdims=True)
@@ -405,7 +433,7 @@
         @pl.when(ends[s])
         def _(s=s):
             arrive(next_final, next_recv)
-            final_source(s, 2, FINALS)
+            final_source(s, 1, FINALS)
 
     sums_middle(partial, parts, part_mid, part_end, rs_send.at[0], rs_recv.at[0])
     plane_arrive(top_stats, top_recv)
@@ -466,6 +494,7 @@
     gather_middle(here, ag_send.at[0], ag_recv.at[0])
     arrive(normed.at[opp, y, x], opp_recv)
     gather_start(there, ag_send.at[1], ag_recv.at[1])
+    turned[...] = hidden[...].T
     chain(PACE[4])
     gather_middle(there, ag_send.at[1], ag_recv.at[1])
     chain(PACE[5])
@@ -477,35 +506,50 @@
     own_head.wait()
     own_final.wait()
 
-    def multiply(block, first):
+    def multiply(block, lo, hi, spans=((0, BLOCK),), first=False):
         def go(n):
             at = aligned(n * 256, 256)
-            value = jnp.dot(
-                normed[block].reshape(TOKENS, BLOCK), heads[block, :, at], preferred_element_type=f32
-            )
+            value = None
+            for a, b in spans:
+                term = jnp.dot(
+                    normed[block, :, :, :, a:b].reshape(TOKENS, b - a), heads[block, a:b, at],
+                    preferred_element_type=f32,
+                )
+                value = term if value is None else value + term
             if first:
                 logits[:, at] = value
             else:
                 logits[:, at] += value
 
-        each(0, QUARTER // 256, go)
-
-    multiply(d, True)
-    chain(PACE[7])
-    arrive(normed.at[sib], sib_recv.at[0])
-    arrive(heads.at[sib], head_recv)
-    multiply(sib, False)
-    chain(1)
-    start_each(HALF_COLUMN, final_copy, fin_send, target.at[own_rows_final, :])
-    multiply(opp, False)
-    arrive(normed.at[opp_sib], sib_recv.at[1])
+        each(lo, hi, go)
 
     def passed(k):
         for s in (0, 1):
             arrive(heads.at[opp_sib, rows_of(s, k), :], pass_recv.at[s, k])
 
-    each(0, CHUNKS, passed)
-    multiply(opp_sib, False)
+    EARLY = CHUNKS // 2
+    early = ((0, HALF // 2), (HALF, HALF + HALF // 2))
+    late = ((HALF // 2, HALF), (HALF + HALF // 2, BLOCK))
+    multiply(d, 0, 2, first=True)
+    chain(PACE[7])
+    multiply(d, 2, 4, first=True)
+    arrive(normed.at[sib], sib_recv.at[0])
+    arrive(heads.at[sib], head_recv)
+    chain(PACE[8])
+    multiply(sib, 0, 2)
+    chain(PACE[9])
+    multiply(sib, 2, 4)
+    chain(PACE[10])
+    multiply(opp, 0, 4, early)
+    chain(PACE[11])
+    arrive(normed.at[opp_sib], sib_recv.at[1])
+    each(0, EARLY, passed)
+    multiply(opp_sib, 0, 4, early)
+    chain(1)
+    start_each(HALF_COLUMN, final_copy, fin_send, target.at[own_rows_final, :])
+    multiply(opp, 0, 4, late)
+    each(EARLY, CHUNKS, passed)
+    multiply(opp_sib, 0, 4, late)
 
     for t in range(TOKENS // TILE):
         have = logits[t * TILE:(t + 1) * TILE, :]
@@ -567,44 +611,37 @@
         )
         cross[...] += jnp.sum(want * (wanted - have), axis=0, keepdims=True)
 
-    def back(block, write):
+    def back(block, lo, hi, write):
         def go(n):
-            at = aligned(n * 256, 256)
             write(
-                at,
+                n,
                 lax.dot_general(
-                    grads[...], heads[block, at, :], (((1,), (1,)), ((), ())),
+                    grads[...], heads[block, aligned(n * 256, 256), :], (((1,), (1,)), ((), ())),
                     preferred_element_type=f32,
                 ),
             )
 
-        each(0, BLOCK // 256, go)
-
-    def crossing_copy(i):
-        return remote(crossing.at[i], crossed.at[i], gx_send.at[i], gx_recv.at[i], l, v, sib)
-
-    for i, block in ((0, opp_sib), (1, sib)):
-        def to_crossing(at, value, i=i):
-            crossing[i, :, at] = value.astype(bf16)
-
-        back(block, to_crossing)
-        crossing_copy(i).start()
-        leaving.append(crossing_copy(i).wait_send)
-
-    for i, block in ((0, opp), (1, d)):
-        def to_logits(at, value):
-            logits[:, at] = value
-
-        back(block, to_logits)
-        arrive(crossed.at[i], gx_recv.at[i])
-
-        def add_rows(t, i=i):
-            at = aligned(t * TILE, TILE)
-            value = (logits[at, :] + crossed[i, at, :].astype(f32)).astype(bf16)
-            summing[i, t] = value.reshape(SIDE, ROWS, BLOCK)
-
-        each(0, TOKENS // TILE, add_rows)
-        sums_start(summing.at[i], sum_parts.at[i], rs_send.at[1 + i], rs_recv.at[1 + i])
+        each(lo, hi, go)
+
+    def crossing_copy(i, n):
+        return remote(crossing.at[i, n], crossed.at[i, n], gx_send.at[i, n], gx_recv.at[i, n], l, v, sib)
+
+    for i, (theirs, ours) in enumerate(((opp_sib, opp), (sib, d))):
+        def to_crossing(n, value, i=i):
+            crossing[i, n] = value.astype(bf16)
+            crossing_copy(i, n).start()
+
+        def to_summing(n, value, i=i):
+            arrive(crossed.at[i, n], gx_recv.at[i, n])
+            value = (value + crossed[i, n].astype(f32)).astype(bf16)
+            summing[i, :, :, :, aligned(n * 256, 256)] = value.reshape(SIDE, SIDE, ROWS, 256)
+
+        back(theirs, 0, 4, to_crossing)
+        leaving.append(lambda i=i: each(0, 4, lambda n: crossing_copy(i, n).wait_send()))
+        back(ours, 0, 2, to_summing)
+        sums_start(summing.at[i], sum_parts.at[i], rs_send.at[1 + i], rs_recv.at[1 + i], (0,))
+        back(ours, 2, 4, to_summing)
+        sums_start(summing.at[i], sum_parts.at[i], rs_send.at[1 + i], rs_recv.at[1 + i], (1,))
 
     for t in range(BLOCKS):
         crosses[v, t:t + 1, :] = inner[t * TILE:(t + 1) * TILE, :].T[0:1, :]
@@ -647,11 +684,9 @@
     drain()
 
 
-def products(hidden, grad, divergence, weights_out, offsets_out, div_out):
+def products(turned, grad, divergence, weights_out, offsets_out, div_out):
     value = grad[...].reshape(TOKENS, grad.shape[-1])
-    weights_out[0] = lax.dot_general(
-        hidden[...], value, (((0,), (0,)), ((), ())), preferred_element_type=f32
-    )
+    weights_out[0] = jnp.dot(turned[...], value, preferred_element_type=f32)
     offsets_out[...] = jnp.sum(value.astype(f32), axis=0, keepdims=True)
     div_out[0] = divergence[0]
 
@@ -663,17 +698,21 @@
     anywhere = pl.BlockSpec(memory_space=pl.ANY)
     width = hidden.shape[1]
     smem = pl.BlockSpec(memory_space=pltpu.SMEM)
-    grad, divergence = pl.pallas_call(
+    grad, turned, divergence = pl.pallas_call(
         kernel,
         out_shape=[
             jax.ShapeDtypeStruct((SIDE, SIDE, ROWS, BLOCK), bf16),
+            jax.ShapeDtypeStruct((width, TOKENS), bf16),
             jax.ShapeDtypeStruct((1,), f32),
         ],
-        in_specs=[in_vmem] * 4 + [anywhere] * 2,
-        out_specs=[in_vmem, smem],
+        in_specs=[anywhere] * 6,
+        out_specs=[in_vmem, in_vmem, smem],
         scratch_shapes=[
-            vmem((BLOCKS, BLOCK, QUARTER), bf16),
-            vmem((BLOCK, QUARTER), bf16),
+            vmem((TOKENS, width), bf16),
+            vmem((width, BLOCK), bf16),
+            vmem((1, BLOCK), f32),
+            vmem((1, BLOCK), f32),
+            vmem((BLOCKS + 1, BLOCK, QUARTER), bf16),
             vmem((BLOCKS, SIDE, SIDE, ROWS, BLOCK), bf16),
             vmem((SIDE, SIDE, ROWS, BLOCK), f32),
             vmem((TOKENS, QUARTER), bf16),
@@ -692,8 +731,8 @@
             vmem((GROUPS, 8, TILE), f32),
             vmem((BLOCKS, 8, TILE), f32),
             vmem((TOKENS, QUARTER), bf16),
-            vmem((2, TOKENS, BLOCK), bf16),
-            vmem((2, TOKENS, BLOCK), bf16),
+            vmem((2, 4, TOKENS, 256), bf16),
+            vmem((2, 4, TOKENS, 256), bf16),
             vmem((2, SIDE, SIDE, ROWS, BLOCK), bf16),
             vmem((2, SIDE, SIDE, ROWS, HALF), f32),
             vmem((2, SIDE, ROWS, HALF), f32),
@@ -722,11 +761,11 @@
             dma((BLOCKS,)), dma((BLOCKS,)),
             dma((GROUPS,)), dma((GROUPS,)),
             dma((BLOCKS,)), dma((BLOCKS,)),
-            dma((2,)), dma((2,)),
+            dma((2, 4)), dma((2, 4)),
             dma((3, 4, SIDE)), dma((3, 4, SIDE)),
             dma((3, 4, SIDE)), dma((3, 4, SIDE)),
             dma, dma,
-            dma((3,)),
+            dma((7,)),
         ],
         compiler_params=pltpu.CompilerParams(
             collective_id=0, has_side_effects=True, vmem_limit_bytes=56 * 1024 * 1024
@@ -743,7 +782,7 @@
         ],
         grid=(BLOCK // tile,),
         in_specs=[
-            pl.BlockSpec((TOKENS, width), lambda n: (0, 0)),
+            pl.BlockSpec((width, TOKENS), lambda n: (0, 0)),
             pl.BlockSpec((SIDE, SIDE, ROWS, tile), lambda n: (0, 0, 0, n)),
             smem,
         ],
@@ -753,7 +792,7 @@
             smem,
         ],
         name="products",
-    )(hidden, grad, divergence)
+    )(turned, grad, divergence)
 
 
 def shards(hidden, translator, bias, gain, head, final_logits):

time: 153 us -> 146 us (0.954); the launches traced: 150 us -> 146 us
  Pallas kernels: 149 us -> 146 us
    pallas_call x1, Pallas kernels: 145 us -> 141 us  [run(): pl.pallas_call(kernel, out_shape=[jax.ShapeDtypeStruct((SIDE, SIDE, ROWS,...]
where the time goes in v5:
time: 146 us
  Pallas kernels  146 us (100%)
    pallas_call x1, Pallas kernels, run(): pl.pallas_call(kernel, out_shape=[jax.ShapeDtypeStruct((SIDE, SIDE, ROWS,...  141 us
    pallas_call x1, Pallas kernels, run(): pl.pallas_call(products, out_shape=[jax.ShapeDtypeStruct((1, width, BLOCK...  4.53 us

profile of v5, /device:TPU:1, one launch (start us, length us, event | category | flops | bytes accessed | tf_op | source)
XLA Modules:
  0.0 146.2 jit_solution(1909922415203597875)
XLA Ops:
  0.6 141.0 %lens.1 = (bf16[4,4,32,1024]{3,2,1,0:T(8,128)(2,1)}, bf16[256,512]{1,0:T(8,128)(2,1)}, f32[1]{0:T(128)}) custom-call(bf16[512,256]{1,0:T(8,128)(2,1)} %bitcast.5, bf16[256,1024]{1,0:T(8,128)(2,1)} %bitcast.4, f32[1,1024]{1,0:T(1,128)} %bias_hbm.1, f32[1,1024]{1,0:T(1,128)} %bitcast.7, bf16[1024,4096]{1,0:T(8,128)(2,1)} %head.1, bf16[32,4096]{1,0:T(8,128)(2,1)} %bitcast.6), custom_call_target="tpu_custom_call" | custom-call | tf_op jit(solution)/shard_map/lens/pallas_call | solution.py:701
  141.6 4.5 %products.1 = (f32[1,256,1024]{2,1,0:T(8,128)}, f32[1,1024]{1,0:T(1,128)}, f32[1]{0:T(128)}) custom-call(bf16[256,512]{1,0:T(8,128)(2,1)} %get-tuple-element.6.turned, bf16[4,4,32,1024]{3,2,1,0:T(8,128)(2,1)} %get-tuple-element.7.grad, f32[1]{0:T(128)} %get-tuple-element.8.divergence), custom_call_target="tpu_custom_call" | custom-call | tf_op jit(solution)/shard_map/products/pallas_call | solution.py:776

commit v6 on v5

--- a/solution.py
+++ b/solution.py
@@ -44,7 +44,7 @@
     hidden_hbm, translator_hbm, bias_hbm, gain_hbm, head, final, gathered_grad, turned, div_out,
     hidden, translator, bias, gain,
     heads, normed, partial, target, final_own, pad, scaled, squares, logits,
-    top_stats, want_lse, stats, stats2, lse, cross, inner, crosses, crosses2, grads, crossing, crossed, summing,
+    top_stats, want_lse, stats, stats2, lse, cross, crosses, crosses2, grads, crossing, crossed, summing,
     parts, part_mid, part_end, sum_parts, sum_mid, sum_end, half_sum, other_sum, finals,
     next_final, passing_final,
     chain_send, chain_recv, pass_send, pass_recv, fchain_send, fchain_recv, fpass_send, fpass_recv,
@@ -396,6 +396,9 @@
     @pl.when(inner_layer)
     def _():
         next_copy.start()
+        each(1, HALF_COLUMN, lambda k: final_copy(k).start())
+
+    leaving.append(lambda: each(1, HALF_COLUMN, lambda k: sent(target.at[own_rows_final, :], fin_send.at[k])))
 
     source(0)
     source(1)
@@ -436,21 +439,6 @@
             final_source(s, 1, FINALS)
 
     sums_middle(partial, parts, part_mid, part_end, rs_send.at[0], rs_recv.at[0])
-    plane_arrive(top_stats, top_recv)
-    all_top = jnp.max(top_stats[:, 0:1, :], axis=0)
-    all_sum = jnp.sum(top_stats[:, 1:2, :] * jnp.exp(top_stats[:, 0:1, :] - all_top[None]), axis=0)
-    row_lse = all_top + jnp.log(jnp.where(own_lanes[0:1, :], all_sum, 1.0))
-    want_lse[column] = jnp.broadcast_to(jnp.where(own_lanes[0:1, :], row_lse, 0.0), (8, TILE))
-
-    def want_copy(k):
-        m = in_column(k)
-        return remote(
-            want_lse.at[column], want_lse.at[column], wl_send.at[k], wl_recv.at[column],
-            lax.div(m, BLOCKS), v, lax.rem(m, BLOCKS),
-        )
-
-    start_each(NCOL, want_copy, wl_send, want_lse.at[0])
-
     chain(PACE[1])
     value_left, value_right = sums_end(part_mid, part_end, rs_recv.at[0])
     scaled[:, left] = value_left + bias[:, left]
@@ -497,6 +485,20 @@
     turned[...] = hidden[...].T
     chain(PACE[4])
     gather_middle(there, ag_send.at[1], ag_recv.at[1])
+    plane_arrive(top_stats, top_recv)
+    all_top = jnp.max(top_stats[:, 0:1, :], axis=0)
+    all_sum = jnp.sum(top_stats[:, 1:2, :] * jnp.exp(top_stats[:, 0:1, :] - all_top[None]), axis=0)
+    row_lse = all_top + jnp.log(jnp.where(own_lanes[0:1, :], all_sum, 1.0))
+    want_lse[column] = jnp.broadcast_to(jnp.where(own_lanes[0:1, :], row_lse, 0.0), (8, TILE))
+
+    def want_copy(k):
+        m = in_column(k)
+        return remote(
+            want_lse.at[column], want_lse.at[column], wl_send.at[k], wl_recv.at[column],
+            lax.div(m, BLOCKS), v, lax.rem(m, BLOCKS),
+        )
+
+    start_each(NCOL, want_copy, wl_send, want_lse.at[0])
     chain(PACE[5])
     gather_end(here, ag_recv.at[0])
     to_sibling(d, 0)
@@ -546,7 +548,10 @@
     each(0, EARLY, passed)
     multiply(opp_sib, 0, 4, early)
     chain(1)
-    start_each(HALF_COLUMN, final_copy, fin_send, target.at[own_rows_final, :])
+    @pl.when(jnp.logical_not(inner_layer))
+    def _():
+        each(1, HALF_COLUMN, lambda k: final_copy(k).start())
+
     multiply(opp, 0, 4, late)
     each(EARLY, CHUNKS, passed)
     multiply(opp_sib, 0, 4, late)
@@ -596,20 +601,15 @@
     top, total = merge(stats2)
     lse[0:4, :] = top + jnp.log(total)
 
-    cross[...] = jnp.zeros((1, QUARTER), f32)
+    def lse_columns(t):
+        have_lse = jnp.broadcast_to(lse[t:t + 1, :], (TILE, TILE)).T[:, 0:1]
+        return have_lse, jnp.broadcast_to(lse[4 + t:5 + t, :], (TILE, TILE)).T[:, 0:1]
+
     for t in range(BLOCKS):
         at = pl.ds(t * TILE, TILE)
-        have_lse = jnp.broadcast_to(lse[t:t + 1, :], (TILE, TILE)).T[:, 0:1]
-        target_lse = jnp.broadcast_to(lse[4 + t:5 + t, :], (TILE, TILE)).T[:, 0:1]
-        wanted = target[at, :].astype(f32)
-        have = logits[at, :]
-        want = jnp.exp(wanted - target_lse)
-        grad = (jnp.exp(have - have_lse) - want).astype(bf16)
-        grads[at, :] = grad
-        inner[at, :] = jnp.broadcast_to(
-            jnp.sum(grad.astype(f32) * have, axis=1, keepdims=True), (TILE, TILE)
-        )
-        cross[...] += jnp.sum(want * (wanted - have), axis=0, keepdims=True)
+        have_lse, target_lse = lse_columns(t)
+        want = jnp.exp(target[at, :].astype(f32) - target_lse)
+        grads[at, :] = (jnp.exp(logits[at, :] - have_lse) - want).astype(bf16)
 
     def back(block, lo, hi, write):
         def go(n):
@@ -643,8 +643,15 @@
         back(ours, 2, 4, to_summing)
         sums_start(summing.at[i], sum_parts.at[i], rs_send.at[1 + i], rs_recv.at[1 + i], (1,))
 
+    cross[...] = jnp.zeros((1, QUARTER), f32)
     for t in range(BLOCKS):
-        crosses[v, t:t + 1, :] = inner[t * TILE:(t + 1) * TILE, :].T[0:1, :]
+        at = pl.ds(t * TILE, TILE)
+        wanted = target[at, :].astype(f32)
+        have = logits[at, :]
+        want = jnp.exp(wanted - lse_columns(t)[1])
+        cross[...] += jnp.sum(want * (wanted - have), axis=0, keepdims=True)
+        inner = jnp.sum(grads[at, :].astype(f32) * have, axis=1, keepdims=True)
+        crosses[v, t:t + 1, :] = jnp.broadcast_to(inner, (TILE, TILE)).T[0:1, :]
     crosses[v, 4:8, :] = jnp.broadcast_to(jnp.sum(cross[...], axis=1, keepdims=True), (4, 128))
     start_each(GROUPS, plane_copy(crosses, cr_send, cr_recv), cr_send, crosses.at[0])
 
@@ -684,11 +691,30 @@
     drain()
 
 
-def products(turned, grad, divergence, weights_out, offsets_out, div_out):
-    value = grad[...].reshape(TOKENS, grad.shape[-1])
-    weights_out[0] = jnp.dot(turned[...], value, preferred_element_type=f32)
-    offsets_out[...] = jnp.sum(value.astype(f32), axis=0, keepdims=True)
+def products(
+    turned_in, grad_in, divergence, weights_out, offsets_out, div_out, turned, grad, weights, in_sem, out_sem
+):
+    tiles, tile = grad.shape[0], grad.shape[-1]
+
+    def part(n):
+        return pl.ds(n * tile, tile)
+
+    whole = pltpu.make_async_copy(turned_in, turned, in_sem.at[tiles])
+    whole.start()
+    ins = [pltpu.make_async_copy(grad_in.at[:, :, :, part(n)], grad.at[n], in_sem.at[n]) for n in range(tiles)]
+    outs = [pltpu.make_async_copy(weights.at[n], weights_out.at[0, :, part(n)], out_sem.at[n]) for n in range(tiles)]
+    for copy in ins:
+        copy.start()
+    whole.wait()
+    for n in range(tiles):
+        ins[n].wait()
+        value = grad[n].reshape(TOKENS, tile)
+        weights[n] = jnp.dot(turned[...], value, preferred_element_type=f32)
+        outs[n].start()
+        offsets_out[:, part(n)] = jnp.sum(value.astype(f32), axis=0, keepdims=True)
     div_out[0] = divergence[0]
+    for copy in outs:
+        copy.wait()
 
 
 def run(hidden, translator, bias, gain, head, final):
@@ -727,7 +753,6 @@
             vmem((BLOCKS, 8, TILE), f32),
             vmem((8, TILE), f32),
             vmem((1, QUARTER), f32),
-            vmem((TOKENS, TILE), f32),
             vmem((GROUPS, 8, TILE), f32),
             vmem((BLOCKS, 8, TILE), f32),
             vmem((TOKENS, QUARTER), bf16),
@@ -780,16 +805,14 @@
             jax.ShapeDtypeStruct((1, BLOCK), f32),
             jax.ShapeDtypeStruct((1,), f32),
         ],
-        grid=(BLOCK // tile,),
-        in_specs=[
-            pl.BlockSpec((width, TOKENS), lambda n: (0, 0)),
-            pl.BlockSpec((SIDE, SIDE, ROWS, tile), lambda n: (0, 0, 0, n)),
-            smem,
-        ],
-        out_specs=[
-            pl.BlockSpec((1, width, tile), lambda n: (0, 0, n)),
-            pl.BlockSpec((1, tile), lambda n: (0, n)),
-            smem,
+        in_specs=[anywhere, anywhere, smem],
+        out_specs=[anywhere, in_vmem, smem],
+        scratch_shapes=[
+            vmem((width, TOKENS), bf16),
+            vmem((BLOCK // tile, SIDE, SIDE, ROWS, tile), bf16),
+            vmem((BLOCK // tile, width, tile), f32),
+            dma((BLOCK // tile + 1,)),
+            dma((BLOCK // tile,)),
         ],
         name="products",
     )(turned, grad, divergence)

time: 146 us -> 144 us (0.986)
  Pallas kernels: 146 us -> 143 us
    pallas_call x1, Pallas kernels: 141 us -> 139 us  [run(): pl.pallas_call(kernel, out_shape=[jax.ShapeDtypeStruct((SIDE, SIDE, ROWS,...]
where the time goes in v6:
time: 144 us
  Pallas kernels  143 us (99%)
    pallas_call x1, Pallas kernels, run(): pl.pallas_call(kernel, out_shape=[jax.ShapeDtypeStruct((SIDE, SIDE, ROWS,...  139 us
    pallas_call x1, Pallas kernels, run(): pl.pallas_call(products, out_shape=[jax.ShapeDtypeStruct((1, width, BLOCK...  4.18 us

profile of v6, /device:TPU:1, one launch (start us, length us, event | category | flops | bytes accessed | tf_op | source)
XLA Modules:
  0.0 143.9 jit_solution(1467393949799394653)
XLA Ops:
  0.6 138.9 %lens.1 = (bf16[4,4,32,1024]{3,2,1,0:T(8,128)(2,1)}, bf16[256,512]{1,0:T(8,128)(2,1)}, f32[1]{0:T(128)}) custom-call(bf16[512,256]{1,0:T(8,128)(2,1)} %bitcast.5, bf16[256,1024]{1,0:T(8,128)(2,1)} %bitcast.4, f32[1,1024]{1,0:T(1,128)} %bias_hbm.1, f32[1,1024]{1,0:T(1,128)} %bitcast.7, bf16[1024,4096]{1,0:T(8,128)(2,1)} %head.1, bf16[32,4096]{1,0:T(8,128)(2,1)} %bitcast.6), custom_call_target="tpu_custom_call" | custom-call | tf_op jit(solution)/shard_map/lens/pallas_call | solution.py:727
  139.5 4.2 %products.1 = (f32[1,256,1024]{2,1,0:T(8,128)}, f32[1,1024]{1,0:T(1,128)}, f32[1]{0:T(128)}) custom-call(bf16[256,512]{1,0:T(8,128)(2,1)} %get-tuple-element.6.turned_in, bf16[4,4,32,1024]{3,2,1,0:T(8,128)(2,1)} %get-tuple-element.7.grad_in, f32[1]{0:T(128)} %get-tuple-element.8.divergence), custom_call_target="tpu_custom_call" | custom-call | tf_op jit(solution)/shard_map/products/pallas_call | solution.py:801

commit v7 on v6

--- a/solution.py
+++ b/solution.py
@@ -510,7 +510,7 @@
 
     def multiply(block, lo, hi, spans=((0, BLOCK),), first=False):
         def go(n):
-            at = aligned(n * 256, 256)
+            at = aligned(n * HALF, HALF)
             value = None
             for a, b in spans:
                 term = jnp.dot(
@@ -532,29 +532,29 @@
     EARLY = CHUNKS // 2
     early = ((0, HALF // 2), (HALF, HALF + HALF // 2))
     late = ((HALF // 2, HALF), (HALF + HALF // 2, BLOCK))
-    multiply(d, 0, 2, first=True)
+    multiply(d, 0, 1, first=True)
     chain(PACE[7])
-    multiply(d, 2, 4, first=True)
+    multiply(d, 1, 2, first=True)
     arrive(normed.at[sib], sib_recv.at[0])
     arrive(heads.at[sib], head_recv)
     chain(PACE[8])
-    multiply(sib, 0, 2)
+    multiply(sib, 0, 1)
     chain(PACE[9])
-    multiply(sib, 2, 4)
+    multiply(sib, 1, 2)
     chain(PACE[10])
-    multiply(opp, 0, 4, early)
+    multiply(opp, 0, 2, early)
     chain(PACE[11])
     arrive(normed.at[opp_sib], sib_recv.at[1])
     each(0, EARLY, passed)
-    multiply(opp_sib, 0, 4, early)
+    multiply(opp_sib, 0, 2, early)
     chain(1)
     @pl.when(jnp.logical_not(inner_layer))
     def _():
         each(1, HALF_COLUMN, lambda k: final_copy(k).start())
 
-    multiply(opp, 0, 4, late)
+    multiply(opp, 0, 2, late)
     each(EARLY, CHUNKS, passed)
-    multiply(opp_sib, 0, 4, late)
+    multiply(opp_sib, 0, 2, late)
 
     for t in range(TOKENS // TILE):
         have = logits[t * TILE:(t + 1) * TILE, :]
@@ -616,7 +616,7 @@
             write(
                 n,
                 lax.dot_general(
-                    grads[...], heads[block, aligned(n * 256, 256), :], (((1,), (1,)), ((), ())),
+                    grads[...], heads[block, aligned(n * HALF, HALF), :], (((1,), (1,)), ((), ())),
                     preferred_element_type=f32,
                 ),
             )
@@ -628,19 +628,21 @@
 
     for i, (theirs, ours) in enumerate(((opp_sib, opp), (sib, d))):
         def to_crossing(n, value, i=i):
-            crossing[i, n] = value.astype(bf16)
-            crossing_copy(i, n).start()
+            for m in (0, 1):
+                crossing[i, 2 * n + m] = value[:, m * 256:(m + 1) * 256].astype(bf16)
+                crossing_copy(i, 2 * n + m).start()
 
         def to_summing(n, value, i=i):
-            arrive(crossed.at[i, n], gx_recv.at[i, n])
-            value = (value + crossed[i, n].astype(f32)).astype(bf16)
-            summing[i, :, :, :, aligned(n * 256, 256)] = value.reshape(SIDE, SIDE, ROWS, 256)
-
-        back(theirs, 0, 4, to_crossing)
+            for m in (0, 1):
+                arrive(crossed.at[i, 2 * n + m], gx_recv.at[i, 2 * n + m])
+                total = (value[:, m * 256:(m + 1) * 256] + crossed[i, 2 * n + m].astype(f32)).astype(bf16)
+                summing[i, :, :, :, aligned(n * HALF + m * 256, 256)] = total.reshape(SIDE, SIDE, ROWS, 256)
+
+        back(theirs, 0, 2, to_crossing)
         leaving.append(lambda i=i: each(0, 4, lambda n: crossing_copy(i, n).wait_send()))
-        back(ours, 0, 2, to_summing)
+        back(ours, 0, 1, to_summing)
         sums_start(summing.at[i], sum_parts.at[i], rs_send.at[1 + i], rs_recv.at[1 + i], (0,))
-        back(ours, 2, 4, to_summing)
+        back(ours, 1, 2, to_summing)
         sums_start(summing.at[i], sum_parts.at[i], rs_send.at[1 + i], rs_recv.at[1 + i], (1,))
 
     cross[...] = jnp.zeros((1, QUARTER), f32)

time: 144 us -> 143 us (level)
  no operation moved by 1% of the time
where the time goes in v7:
time: 143 us
  Pallas kernels  142 us (99%)
    pallas_call x1, Pallas kernels, run(): pl.pallas_call(kernel, out_shape=[jax.ShapeDtypeStruct((SIDE, SIDE, ROWS,...  138 us
    pallas_call x1, Pallas kernels, run(): pl.pallas_call(products, out_shape=[jax.ShapeDtypeStruct((1, width, BLOCK...  4.18 us

profile of v7, /device:TPU:1, one launch (start us, length us, event | category | flops | bytes accessed | tf_op | source)
XLA Modules:
  0.0 142.9 jit_solution(12931847572351770332)
XLA Ops:
  0.6 137.9 %lens.1 = (bf16[4,4,32,1024]{3,2,1,0:T(8,128)(2,1)}, bf16[256,512]{1,0:T(8,128)(2,1)}, f32[1]{0:T(128)}) custom-call(bf16[512,256]{1,0:T(8,128)(2,1)} %bitcast.5, bf16[256,1024]{1,0:T(8,128)(2,1)} %bitcast.4, f32[1,1024]{1,0:T(1,128)} %bias_hbm.1, f32[1,1024]{1,0:T(1,128)} %bitcast.7, bf16[1024,4096]{1,0:T(8,128)(2,1)} %head.1, bf16[32,4096]{1,0:T(8,128)(2,1)} %bitcast.6), custom_call_target="tpu_custom_call" | custom-call | tf_op jit(solution)/shard_map/lens/pallas_call | solution.py:729
  138.6 4.2 %products.1 = (f32[1,256,1024]{2,1,0:T(8,128)}, f32[1,1024]{1,0:T(1,128)}, f32[1]{0:T(128)}) custom-call(bf16[256,512]{1,0:T(8,128)(2,1)} %get-tuple-element.6.turned_in, bf16[4,4,32,1024]{3,2,1,0:T(8,128)(2,1)} %get-tuple-element.7.grad_in, f32[1]{0:T(128)} %get-tuple-element.8.divergence), custom_call_target="tpu_custom_call" | custom-call | tf_op jit(solution)/shard_map/products/pallas_call | solution.py:803

commit v8 on v7

--- a/solution.py
+++ b/solution.py
@@ -111,6 +111,20 @@
     def own_rows(p):
         return aligned(p * ROWS, ROWS)
 
+    barrier = pltpu.get_barrier_semaphore()
+
+    def greet_plane(k):
+        pl.semaphore_signal(barrier, inc=1, device_id=(l, in_plane(k), d), device_id_type=MESH)
+
+    def greet_column(k):
+        m = in_column(k)
+        pl.semaphore_signal(
+            barrier, inc=1, device_id=(lax.div(m, BLOCKS), v, lax.rem(m, BLOCKS)), device_id_type=MESH
+        )
+
+    each(1, GROUPS, greet_plane)
+    each(1, NCOL, greet_column)
+
     staged = [
         pltpu.make_async_copy(src, dst, local_sem.at[3 + n])
         for n, (src, dst) in enumerate(
@@ -126,20 +140,6 @@
     own_final.start()
     whole_final = pltpu.make_async_copy(final, final_own, local_sem.at[2])
     whole_final.start()
-
-    barrier = pltpu.get_barrier_semaphore()
-
-    def greet_plane(k):
-        pl.semaphore_signal(barrier, inc=1, device_id=(l, in_plane(k), d), device_id_type=MESH)
-
-    def greet_column(k):
-        m = in_column(k)
-        pl.semaphore_signal(
-            barrier, inc=1, device_id=(lax.div(m, BLOCKS), v, lax.rem(m, BLOCKS)), device_id_type=MESH
-        )
-
-    each(1, GROUPS, greet_plane)
-    each(1, NCOL, greet_column)
 
     def product(n):
         at = aligned(n * 256, 256)

time: 143 us -> 143 us (level)
  no operation moved by 1% of the time
where the time goes in v8:
time: 143 us; the launch traced here: 142 us
  Pallas kernels  142 us (99%)
    pallas_call x1, Pallas kernels, run(): pl.pallas_call(kernel, out_shape=[jax.ShapeDtypeStruct((SIDE, SIDE, ROWS,...  137 us
    pallas_call x1, Pallas kernels, run(): pl.pallas_call(products, out_shape=[jax.ShapeDtypeStruct((1, width, BLOCK...  4.18 us

profile of v8, /device:TPU:1, one launch (start us, length us, event | category | flops | bytes accessed | tf_op | source)
XLA Modules:
  0.0 142.4 jit_solution(8252456046616518440)
XLA Ops:
  0.6 137.5 %lens.1 = (bf16[4,4,32,1024]{3,2,1,0:T(8,128)(2,1)}, bf16[256,512]{1,0:T(8,128)(2,1)}, f32[1]{0:T(128)}) custom-call(bf16[512,256]{1,0:T(8,128)(2,1)} %bitcast.5, bf16[256,1024]{1,0:T(8,128)(2,1)} %bitcast.4, f32[1,1024]{1,0:T(1,128)} %bias_hbm.1, f32[1,1024]{1,0:T(1,128)} %bitcast.7, bf16[1024,4096]{1,0:T(8,128)(2,1)} %head.1, bf16[32,4096]{1,0:T(8,128)(2,1)} %bitcast.6), custom_call_target="tpu_custom_call" | custom-call | tf_op jit(solution)/shard_map/lens/pallas_call | solution.py:729
  138.1 4.2 %products.1 = (f32[1,256,1024]{2,1,0:T(8,128)}, f32[1,1024]{1,0:T(1,128)}, f32[1]{0:T(128)}) custom-call(bf16[256,512]{1,0:T(8,128)(2,1)} %get-tuple-element.6.turned_in, bf16[4,4,32,1024]{3,2,1,0:T(8,128)(2,1)} %get-tuple-element.7.grad_in, f32[1]{0:T(128)} %get-tuple-element.8.divergence), custom_call_target="tpu_custom_call" | custom-call | tf_op jit(solution)/shard_map/products/pallas_call | solution.py:803
